TPU v7x, 256 devices: a whole 4x4x8 slice. The times are simulated.
256 devices in a mesh: pipe: 32 (over z, x_hi, core), tensor: 8 (over x_lo, y).
Axes of the slice: x: 4 (x_hi: 2, x_lo: 2; x = x_hi * 2 + x_lo), y: 4, z: 8, core: 2. Of those that a mesh axis runs over, the one named last changes fastest.
Arguments:
- hidden: bfloat16 [12288, 14784], P('pipe', 'tensor'), may hold values from -6 to 6
- down_weight: bfloat16 [14784, 4096], P('tensor', 'pipe'), may hold values from -0.046875 to 0.046875
- adapter_in: bfloat16 [16, 14784], P(None, 'tensor'), may hold values from -0.046875 to 0.046875
- adapter_out: bfloat16 [16, 4096], P(None, 'pipe'), may hold values from -0.09375 to 0.09375
- cotangent: bfloat16 [12288, 4096], P('pipe', 'tensor'), may hold values from -6 to 6
Outputs:
- projected: bfloat16 [12288, 4096], P('pipe', 'tensor')
- hidden_gradient: bfloat16 [12288, 14784], P('pipe', 'tensor')
- grad_in: float32 [16, 14784], P(None, 'tensor')
- grad_out: float32 [16, 4096], P(None, 'tensor')
All inputs are finite; a program needn't handle non-finite values.
Results may differ from a plain program's by a relative error of at most 0.0034.
Values may be sent and summed in bfloat16 or wider, within the bound.
No kernel may reach another device: no remote copies, remote signals or barrier semaphores. Data moves between devices by JAX's collectives and lax.ppermute only.
A program may use at most 128 MiB of HBM per device.

v0:
```python
import math

import jax
import jax.numpy as jnp
from jax import lax
from jax.experimental import pallas as pl
from jax.experimental.pallas import tpu as pltpu
from jax.sharding import Mesh, PartitionSpec as P

SCALE = 2.0
PIPE = ("z", "x_hi", "core")
TENSOR = ("x_lo", "y")
NZ, NT, NY = 8, 8, 4
F32, BF16 = jnp.float32, jnp.bfloat16


def swap(x, axis):
    return lax.ppermute(x, axis, [(0, 1), (1, 0)])


def from_offset(x, k):
    return lax.ppermute(x, "z", [((i + k) % NZ, i) for i in range(NZ)])


def from_xor(x, axis, n, k):
    return lax.ppermute(x, axis, [(i ^ k, i) for i in range(n)])


def dot(a, b, ca, cb):
    return lax.dot_general(a, b, (((ca,), (cb,)), ((), ())), preferred_element_type=F32)


together = lax.optimization_barrier


def flip(a, b, bit):
    return [jnp.where(bit == 0, a, b), jnp.where(bit == 0, b, a)]


def groups(x, x_hi, core):
    width = x.shape[1] // 4
    return [
        lax.dynamic_slice_in_dim(x, ((x_hi ^ i) * 2 + (core ^ j)) * width, width, 1)
        for i in range(2)
        for j in range(2)
    ]


def copy_kernel(at, in_ref, out_ref):
    out_ref[...] = in_ref[...]


def reorder(x, at):
    rows, group = x.shape[0], x.shape[1] // at.shape[0]
    return pl.pallas_call(
        copy_kernel,
        out_shape=jax.ShapeDtypeStruct(x.shape, x.dtype),
        grid_spec=pltpu.PrefetchScalarGridSpec(
            num_scalar_prefetch=1,
            grid=at.shape,
            in_specs=[pl.BlockSpec((rows, group), lambda i, at: (0, at[i]))],
            out_specs=pl.BlockSpec((rows, group), lambda i, at: (0, i)),
        ),
        compiler_params=pltpu.CompilerParams(vmem_limit_bytes=8 * 2**20),
        cost_estimate=pl.CostEstimate(flops=0, bytes_accessed=4 * x.size, transcendentals=0),
    )(at, x)


def local(hidden, w, a_in, a_out, cot):
    z, x_hi, core = (lax.axis_index(a) for a in PIPE)
    x_lo, y = (lax.axis_index(a) for a in TENSOR)
    t = x_lo * NY + y
    tokens, units = hidden.shape
    group = w.shape[1]

    all_w = lax.all_gather(w, "z", axis=1, tiled=True)

    def from_quad(x, k):
        return from_xor(x, ("x_hi", "core"), 4, k)

    cot_g = groups(cot, x_hi, core)
    mine = [cot_g[0]] + [from_quad(cot_g[k], k) for k in (2, 1, 3)]
    g = [a_out] + [from_quad(a_out, k) for k in range(1, 4)]
    mine = jnp.concatenate(mine, 0)
    g = jnp.concatenate(g, 1)[None]
    mine, g = together((mine, g))
    cot_t, hidden_own = together((jnp.concatenate([mine, swap(mine, "x_lo")], 1), hidden))
    hidden_x = swap(hidden_own, "x_hi")
    cots = [cot_t] + [from_xor(cot_t, "y", NY, k) for k in range(1, NY)]
    for k in (1, 2, 4):
        g = jnp.concatenate([g, from_offset(g, k)], 0)
    hidden_x, g, cots = together((hidden_x, g, cots))
    hidden_x = jnp.concatenate([hidden, hidden_x], 0)
    all_hidden = jnp.concatenate([hidden_x, swap(hidden_x, "core")], 0)
    cots = jnp.concatenate(cots, 1)

    cot_rel = jnp.concatenate(cot_g, 1)
    factor = lax.dynamic_index_in_dim(g, (t - z) % NZ, 0, keepdims=False)
    x = jnp.concatenate([dot(a_in, hidden, 1, 1), dot(factor, cot_rel, 1, 1)], 0)
    for k in (1, 2, 4):
        x = x + from_xor(x, TENSOR, NT, k)
    ranks = x.astype(BF16)

    cots, all_w, ranks, all_hidden = together((cots, all_w, ranks, all_hidden))
    at = [(x_lo ^ i) * NY + (y ^ k) for k in range(NY) for i in range(2)]
    all_w = reorder(all_w, jnp.stack(at))

    def forward(k):
        return dot(all_hidden, all_w[:, 2 * k * group : 2 * (k + 1) * group], 1, 0).astype(BF16)

    def backward(first, last):
        return dot(cots[first * tokens : last * tokens], all_w, 1, 1)

    got, all_hidden = together((backward(2, 4).astype(BF16), all_hidden))
    got = swap(got, "core")
    shares = {1: forward(1), 3: forward(3)}
    rank, back = ranks[:16], ranks[16:]
    c = SCALE / math.sqrt(tokens * 32)
    grads = jnp.concatenate([c * dot(back, hidden, 1, 0), c * dot(rank, cot, 1, 0)], 1)
    grads = grads + swap(grads, "core")
    rank_x = jnp.concatenate([rank, swap(rank, "x_hi")], 1)
    all_rank = jnp.concatenate([rank_x, swap(rank_x, "core")], 1)
    got, shares, cots, all_hidden, all_rank = together((got, shares, cots, all_hidden, all_rank))
    sent = {k: from_xor(shares[k], "y", NY, k) for k in (1, 3)}
    give = (backward(1, 2) + got[tokens:].astype(F32)).astype(BF16)
    give, all_hidden = together((give, all_hidden))
    last = swap(give, "x_hi")
    shares = {2: forward(2), 0: forward(0)}
    sent[2] = from_xor(shares[2], "y", NY, 2)
    cots, main, last, grads = together((cots, shares[0], last, grads))
    own = backward(0, 1) + got[:tokens].astype(F32) + SCALE * dot(back, a_in, 0, 0)
    for k in (1, 2, 4):
        grads = grads + from_xor(grads, "z", NZ, k)
    grads = grads + swap(grads, "x_hi")
    main, own = together((main, own))

    main = main.astype(F32)
    for k in (1, 3, 2):
        main = main + sent[k].astype(F32)
    main = main[:, :group] + swap(main[:, group:].astype(BF16), "x_lo").astype(F32)
    out = (main + SCALE * dot(all_rank, factor[:, :group], 0, 0)).astype(BF16)
    out = jnp.concatenate([out[: 2 * tokens], swap(out[2 * tokens :], "core")], 1)
    out = jnp.concatenate([out[:tokens], swap(out[tokens:], "x_hi")], 1)
    projected = jnp.concatenate(groups(out, x_hi, core), 1)
    hidden_gradient = (own + last.astype(F32)).astype(BF16)
    return projected, hidden_gradient, grads[:, :units], grads[:, units:]


def solution(mesh):
    fine = Mesh(mesh.devices.reshape(8, 2, 2, 2, 4), PIPE + TENSOR)
    return jax.shard_map(
        local,
        mesh=fine,
        in_specs=(P(PIPE, TENSOR), P(TENSOR, PIPE), P(None, TENSOR), P(None, PIPE), P(PIPE, TENSOR)),
        out_specs=(P(PIPE, TENSOR), P(PIPE, TENSOR), P(None, TENSOR), P(None, TENSOR)),
        check_vma=False,
    )
```

profile of v0, /device:TPU:96, one launch (start us, length us, event | category | flops | bytes accessed | tf_op | source)
XLA Modules:
  0.0 205.8 jit_solution(7299828180768456975)
XLA Ops:
  7.2 0.7 all-gather.2.cloned.1.call-update
  7.9 2.5 %collective-permute-start.5 = (bf16[16,128]{1,0:T(8,128)(2,1)}, bf16[16,128]{1,0:T(8,128)(2,1)S(1)}, u32[]{:S(2)}, u32[]{:S(2)}) collective-permute-start(bf16[16,128]{1,0:T(8,128)(2,1)} %param.8), channel_id=1, source_target_pairs={{24,0},{16,8},{8,16},{0,24},{25,1},{17,9},{9,17},{1,25},{26,2},{18... | collective-permute-start | bytes 12296 | tf_op jit(solution)/shard_map/ppermute | solution.py:26
  10.5 0.7 collective-permute-start.4
  11.4 1.1 constant_dynamic-slice_fusion.3
  12.5 2.8 %collective-permute-start.2 = (bf16[384,128]{1,0:T(8,128)(2,1)S(1)}, bf16[384,128]{1,0:T(8,128)(2,1)S(1)}, u32[]{:S(2)}, u32[]{:S(2)}) collective-permute-start(bf16[384,128]{1,0:T(8,128)(2,1)S(1)} %get-tuple-element.75), channel_id=1, source_target_pairs={{24,0},{16,8},{8,16},{0,24},{25,1},{17,9},{9,17},{1,25},{26,2},{18... | collective-permute-start | bytes 294920 | tf_op jit(solution)/shard_map/ppermute | solution.py:26
  15.3 0.4 collective-permute-start.1
  15.7 0.5 collective-permute-start
  16.2 0.7 maximum_bitcast_fusion
  16.9 1.9 collective-permute-done.2
  18.8 3.2 %collective-permute-done = bf16[384,128]{1,0:T(8,128)(2,1)S(1)} collective-permute-done((bf16[384,128]{1,0:T(8,128)(2,1)S(1)}, bf16[384,128]{1,0:T(8,128)(2,1)S(1)}, u32[]{:S(2)}, u32[]{:S(2)}) %collective-permute-start) | collective-permute-done | bytes 98336 | tf_op jit(solution)/shard_map/ppermute | solution.py:26
  22.0 0.8 collective-permute-start.6
  22.9 9.6 %collective-permute-done.6 = bf16[1536,128]{1,0:T(8,128)(2,1)S(1)} collective-permute-done((bf16[1536,128]{1,0:T(8,128)(2,1)S(1)}, bf16[1536,128]{1,0:T(8,128)(2,1)S(1)}, u32[]{:S(2)}, u32[]{:S(2)}) %collective-permute-start.6) | collective-permute-done | bytes 393248 | tf_op jit(solution)/shard_map/ppermute | solution.py:18
  32.5 2.9 %collective-permute-start.7 = (bf16[384,1848]{0,1:T(8,128)(2,1)S(1)}, bf16[384,1848]{0,1:T(8,128)(2,1)S(1)}, u32[]{:S(2)}, u32[]{:S(2)}) collective-permute-start(bf16[384,1848]{0,1:T(8,128)(2,1)S(1)} %copy-done.2), channel_id=1, source_target_pairs={{0,16},{16,0},{1,17},{17,1},{2,18},{18,2},{3,19},{19,3},{4,20},{20... | collective-permute-start | bytes 4257800 | tf_op jit(solution)/shard_map/ppermute | solution.py:18
  35.4 1.6 collective-permute-start.11
  37.0 2.9 %collective-permute-start.12 = (bf16[1536,256]{1,0:T(8,128)(2,1)S(1)}, bf16[1536,256]{1,0:T(8,128)(2,1)S(1)}, u32[]{:S(2)}, u32[]{:S(2)}) collective-permute-start(bf16[1536,256]{1,0:T(8,128)(2,1)S(1)} %pad_maximum_fusion.3), channel_id=1, source_target_pairs={{2,0},{3,1},{0,2},{1,3},{6,4},{7,5},{4,6},{5,7},{10,8},{11,9},{8,1... | collective-permute-start | bytes 2359304 | tf_op jit(solution)/shard_map/ppermute | solution.py:26
  40.2 5.0 %collective-permute-done.8 = bf16[1,16,512]{2,1,0:T(8,128)(2,1)S(1)} collective-permute-done((bf16[1,16,512]{2,1,0:T(8,128)(2,1)S(1)}, bf16[1,16,512]{2,1,0:T(8,128)(2,1)S(1)}, u32[]{:S(2)}, u32[]{:S(2)}) %collective-permute-start.8) | collective-permute-done | bytes 16416 | tf_op jit(solution)/shard_map/ppermute | solution.py:22
  45.2 7.0 %collective-permute-done.9 = bf16[2,16,512]{2,1,0:T(8,128)(2,1)S(1)} collective-permute-done((bf16[2,16,512]{2,1,0:T(8,128)(2,1)S(1)}, bf16[2,16,512]{2,1,0:T(8,128)(2,1)S(1)}, u32[]{:S(2)}, u32[]{:S(2)}) %collective-permute-start.9) | collective-permute-done | bytes 32800 | tf_op jit(solution)/shard_map/ppermute | solution.py:22
  52.3 3.9 %collective-permute-start.10 = (bf16[4,16,512]{2,1,0:T(8,128)(2,1)S(1)}, bf16[4,16,512]{2,1,0:T(8,128)(2,1)S(1)}, u32[]{:S(2)}, u32[]{:S(2)}) collective-permute-start(bf16[4,16,512]{2,1,0:T(8,128)(2,1)S(1)} %pad_maximum_fusion.9), channel_id=1, source_target_pairs={{128,0},{160,32},{192,64},{224,96},{0,128},{32,160},{64,192},{96,2... | collective-permute-start | bytes 196616 | tf_op jit(solution)/shard_map/ppermute | solution.py:22
  56.2 5.9 %collective-permute-done.10 = bf16[4,16,512]{2,1,0:T(8,128)(2,1)S(1)} collective-permute-done((bf16[4,16,512]{2,1,0:T(8,128)(2,1)S(1)}, bf16[4,16,512]{2,1,0:T(8,128)(2,1)S(1)}, u32[]{:S(2)}, u32[]{:S(2)}) %collective-permute-start.10) | collective-permute-done | bytes 65568 | tf_op jit(solution)/shard_map/ppermute | solution.py:22
  62.2 10.9 %collective-permute-done.12 = bf16[1536,256]{1,0:T(8,128)(2,1)S(1)} collective-permute-done((bf16[1536,256]{1,0:T(8,128)(2,1)S(1)}, bf16[1536,256]{1,0:T(8,128)(2,1)S(1)}, u32[]{:S(2)}, u32[]{:S(2)}) %collective-permute-start.12) | collective-permute-done | bytes 786464 | tf_op jit(solution)/shard_map/ppermute | solution.py:26
  73.1 2.6 %collective-permute-done.13 = bf16[1536,256]{1,0:T(8,128)(2,1)S(1)} collective-permute-done((bf16[1536,256]{1,0:T(8,128)(2,1)S(1)}, bf16[1536,256]{1,0:T(8,128)(2,1)S(1)}, u32[]{:S(2)}, u32[]{:S(2)}) %collective-permute-start.13) | collective-permute-done | bytes 786464 | tf_op jit(solution)/shard_map/ppermute | solution.py:26
  75.6 0.9 copy-done.8
  76.5 1.8 pad_maximum_fusion.2
  78.3 0.3 fusion.32
  78.9 4.1 %collective-permute-done.14 = f32[32,384]{1,0:T(8,128)S(1)} collective-permute-done((f32[32,384]{1,0:T(8,128)S(1)}, f32[32,384]{1,0:T(8,128)S(1)}, u32[]{:S(2)}, u32[]{:S(2)}) %collective-permute-start.14) | collective-permute-done | bytes 49184 | tf_op jit(solution)/shard_map/ppermute | solution.py:26
  83.2 5.5 %collective-permute-done.15 = f32[32,384]{1,0:T(8,128)S(1)} collective-permute-done((f32[32,384]{1,0:T(8,128)S(1)}, f32[32,384]{1,0:T(8,128)S(1)}, u32[]{:S(2)}, u32[]{:S(2)}) %collective-permute-start.15) | collective-permute-done | bytes 49184 | tf_op jit(solution)/shard_map/ppermute | solution.py:26
  88.7 0.9 collective-permute-start.16
  89.6 3.3 %pad_maximum_fusion.1 = bf16[1536,1024]{1,0:T(8,128)(2,1)} fusion(bf16[1536,256]{1,0:T(8,128)(2,1)} %copy-done.8, bf16[1536,256]{1,0:T(8,128)(2,1)} %copy-done.7, bf16[1536,256]{1,0:T(8,128)(2,1)} %copy-done.6, bf16[1536,256]{1,0:T(8,128)(2,1)} %copy-done.3), kind=kLoop, calls=%fused_computation.2 | loop fusion | flops 12582912 | bytes 6291456 | tf_op jit(solution)/shard_map/concatenate | solution.py:95
  93.1 4.7 %pad_maximum_fusion = bf16[1536,1848]{0,1:T(8,128)(2,1)} fusion(bf16[768,1848]{0,1:T(8,128)(2,1)} %collective-permute-done.17, bf16[384,1848]{0,1:T(8,128)(2,1)S(1)} %collective-permute-done.7, bf16[384,1848]{0,1:T(8,128)(2,1)S(1)} %copy-done.2), kind=kLoop, calls=%fused_computation | loop fusion | flops 17031168 | bytes 11354112 | tf_op jit(solution)/shard_map/concatenate | solution.py:94
  97.8 2.1 %copy-done.1 = bf16[1848,1024]{1,0:T(8,128)(2,1)S(1)} copy-done((bf16[1848,1024]{1,0:T(8,128)(2,1)S(1)}, bf16[1848,1024]{1,0:T(8,128)(2,1)}, u32[]{:S(2)}) %copy-start.1) | copy-done | bytes 3784728
  99.9 3.0 %shard_map.84 = bf16[1848,1024]{1,0:T(8,128)(2,1)S(1)} custom-call(s32[8]{0:T(128)S(1)} %stack.35.at, bf16[1848,1024]{1,0:T(8,128)(2,1)S(1)} %copy-done.1), custom_call_target="tpu_custom_call" | custom-call | bytes 7569408 | tf_op jit(solution)/shard_map/pallas_call | solution.py:55
  102.9 3.4 %convolution_convert_fusion = bf16[768,1848]{0,1:T(8,128)(2,1)S(1)} fusion(bf16[1848,1024]{1,0:T(8,128)(2,1)S(1)} %shard_map.84, bf16[1536,1024]{1,0:T(8,128)(2,1)S(1)} %copy-done.4), kind=kOutput, calls=%fused_computation.1 | convolution fusion | flops 2908071936 | bytes 8196096 | tf_op jit(solution)/shard_map/dot_general | solution.py:30
  106.4 1.1 collective-permute-start.19
  107.5 0.5 convolution_multiply_fusion.2
  108.0 1.9 convolution_convert_fusion.4
  109.9 1.9 convolution_convert_fusion.3
  112.3 0.4 collective-permute-start.22
  112.7 0.6 collective-permute-done.20
  113.3 2.2 %fusion.1 = bf16[384,1848]{0,1:T(8,128)(2,1)S(1)} fusion(bf16[1848,1024]{1,0:T(8,128)(2,1)S(1)} %shard_map.84, bf16[768,1848]{0,1:T(8,128)(2,1)S(1)} %collective-permute-done.18, bf16[1536,1024]{1,0:T(8,128)(2,1)S(1)} %copy-done.4), kind=kOutput, calls=%fused_computation.9 | convolution fusion | flops 1455455232 | bytes 7409664 | tf_op jit(solution)/shard_map/dot_general | solution.py:30
  115.5 2.8 %collective-permute-start.21 = (bf16[384,1848]{0,1:T(8,128)(2,1)S(1)}, bf16[384,1848]{0,1:T(8,128)(2,1)S(1)}, u32[]{:S(2)}, u32[]{:S(2)}) collective-permute-start(bf16[384,1848]{0,1:T(8,128)(2,1)S(1)} %fusion.1), channel_id=1, source_target_pairs={{0,16},{16,0},{1,17},{17,1},{2,18},{18,2},{3,19},{19,3},{4,20},{20... | collective-permute-start | bytes 4257800 | tf_op jit(solution)/shard_map/ppermute | solution.py:18
  118.5 1.9 convolution_convert_fusion.1
  120.5 2.9 %collective-permute-start.24 = (bf16[1536,256]{1,0:T(8,128)(2,1)S(1)}, bf16[1536,256]{1,0:T(8,128)(2,1)S(1)}, u32[]{:S(2)}, u32[]{:S(2)}) collective-permute-start(bf16[1536,256]{1,0:T(8,128)(2,1)S(1)} %convolution_convert_fusion.3), channel_id=1, source_target_pairs={{3,0},{2,1},{1,2},{0,3},{7,4},{6,5},{5,6},{4,7},{11,8},{10,9},{9,1... | collective-permute-start | bytes 2359304 | tf_op jit(solution)/shard_map/ppermute | solution.py:26
  123.4 0.5 collective-permute-start.23
  123.9 1.9 convolution_convert_fusion.2
  125.8 24.7 %collective-permute-done.21 = bf16[384,1848]{0,1:T(8,128)(2,1)S(1)} collective-permute-done((bf16[384,1848]{0,1:T(8,128)(2,1)S(1)}, bf16[384,1848]{0,1:T(8,128)(2,1)S(1)}, u32[]{:S(2)}, u32[]{:S(2)}) %collective-permute-start.21) | collective-permute-done | bytes 1419296 | tf_op jit(solution)/shard_map/ppermute | solution.py:18
  150.5 2.3 %convolution_add_fusion = f32[384,1848]{0,1:T(8,128)S(1)} fusion(bf16[1848,1024]{1,0:T(8,128)(2,1)S(1)} %shard_map.84, bf16[768,1848]{0,1:T(8,128)(2,1)S(1)} %collective-permute-done.18, bf16[1536,1024]{1,0:T(8,128)(2,1)S(1)} %copy-done.4), kind=kOutput, calls=%fused_computation.5 | convolution fusion | flops 1454745600 | bytes 8828928 | tf_op jit(solution)/shard_map/dot_general | solution.py:30
  152.8 0.7 fusion
  153.5 4.4 %collective-permute-done.24 = bf16[1536,256]{1,0:T(8,128)(2,1)S(1)} collective-permute-done((bf16[1536,256]{1,0:T(8,128)(2,1)S(1)}, bf16[1536,256]{1,0:T(8,128)(2,1)S(1)}, u32[]{:S(2)}, u32[]{:S(2)}) %collective-permute-start.24) | collective-permute-done | bytes 786464 | tf_op jit(solution)/shard_map/ppermute | solution.py:26
  157.9 0.4 convert_add_fusion
  158.4 1.3 collective-permute-start.26
  159.7 5.4 %collective-permute-done.29 = f32[16,2360]{1,0:T(8,128)S(1)} collective-permute-done((f32[16,2360]{1,0:T(8,128)S(1)}, f32[16,2360]{1,0:T(8,128)S(1)}, u32[]{:S(2)}, u32[]{:S(2)}) %collective-permute-start.29) | collective-permute-done | bytes 151072 | tf_op jit(solution)/shard_map/ppermute | solution.py:26
  165.3 4.0 %collective-permute-done.26 = bf16[1536,128]{1,0:T(8,128)(2,1)S(1)} collective-permute-done((bf16[1536,128]{1,0:T(8,128)(2,1)S(1)}, bf16[1536,128]{1,0:T(8,128)(2,1)S(1)}, u32[]{:S(2)}, u32[]{:S(2)}) %collective-permute-start.26) | collective-permute-done | bytes 393248 | tf_op jit(solution)/shard_map/ppermute | solution.py:18
  169.3 0.3 fusion.8
  169.7 4.3 %collective-permute-done.30 = f32[16,2360]{1,0:T(8,128)S(1)} collective-permute-done((f32[16,2360]{1,0:T(8,128)S(1)}, f32[16,2360]{1,0:T(8,128)S(1)}, u32[]{:S(2)}, u32[]{:S(2)}) %collective-permute-start.30) | collective-permute-done | bytes 151072 | tf_op jit(solution)/shard_map/ppermute | solution.py:26
  174.1 4.5 %collective-permute-start.31 = (f32[16,2360]{1,0:T(8,128)S(1)}, f32[16,2360]{1,0:T(8,128)S(1)}, u32[]{:S(2)}, u32[]{:S(2)}) collective-permute-start(f32[16,2360]{1,0:T(8,128)S(1)} %add.148), channel_id=1, source_target_pairs={{128,0},{160,32},{192,64},{224,96},{0,128},{32,160},{64,192},{96,2... | collective-permute-start | bytes 453128 | tf_op jit(solution)/shard_map/ppermute | solution.py:26
  178.6 8.4 %collective-permute-done.31 = f32[16,2360]{1,0:T(8,128)S(1)} collective-permute-done((f32[16,2360]{1,0:T(8,128)S(1)}, f32[16,2360]{1,0:T(8,128)S(1)}, u32[]{:S(2)}, u32[]{:S(2)}) %collective-permute-start.31) | collective-permute-done | bytes 151072 | tf_op jit(solution)/shard_map/ppermute | solution.py:26
  187.0 1.3 collective-permute-start.32
  188.4 2.4 %collective-permute-start.28 = (bf16[384,256]{1,0:T(8,128)(2,1)S(1)}, bf16[384,256]{1,0:T(8,128)(2,1)S(1)}, u32[]{:S(2)}, u32[]{:S(2)}) collective-permute-start(bf16[384,256]{1,0:T(8,128)(2,1)S(1)} %get-tuple-element.68), channel_id=1, source_target_pairs={{0,16},{16,0},{1,17},{17,1},{2,18},{18,2},{3,19},{19,3},{4,20},{20... | collective-permute-start | bytes 589832 | tf_op jit(solution)/shard_map/ppermute | solution.py:18
  190.8 1.4 add_convert_fusion
  192.2 3.4 %collective-permute-done.32 = f32[16,2360]{1,0:T(8,128)S(1)} collective-permute-done((f32[16,2360]{1,0:T(8,128)S(1)}, f32[16,2360]{1,0:T(8,128)S(1)}, u32[]{:S(2)}, u32[]{:S(2)}) %collective-permute-start.32) | collective-permute-done | bytes 151072 | tf_op jit(solution)/shard_map/ppermute | solution.py:18
  195.6 0.7 slice.92
  196.3 0.7 slice.93
  197.0 1.0 collective-permute-done.28
  198.2 0.8 pad_maximum_fusion.5
  (76 shorter events, 2.9 us)
Async XLA Ops:
  7.2 71.1 %copy-start = (bf16[16,1848]{1,0:T(8,128)(2,1)S(1)}, bf16[16,1848]{1,0:T(8,128)(2,1)}, u32[]{:S(2)}) copy-start(bf16[16,1848]{1,0:T(8,128)(2,1)} %param.7) | copy-start | bytes 177412
  7.2 25.3 %copy-start.2 = (bf16[384,1848]{0,1:T(8,128)(2,1)S(1)}, bf16[384,1848]{0,1:T(8,128)(2,1)}, u32[]{:S(2)}) copy-start(bf16[384,1848]{0,1:T(8,128)(2,1)} %param.5) | copy-start | bytes 4257796
  7.2 90.6 %all-gather.2.cloned.1.call-start = ((), (), s32[]{:S(2)}) async-start(), calls=%async_computation | async-start | bytes 4257792 | tf_op jit(solution)/shard_map/all_gather | solution.py:76
  7.9 7.8 %collective-permute-start.5 = (bf16[16,128]{1,0:T(8,128)(2,1)}, bf16[16,128]{1,0:T(8,128)(2,1)S(1)}, u32[]{:S(2)}, u32[]{:S(2)}) collective-permute-start(bf16[16,128]{1,0:T(8,128)(2,1)} %param.8), channel_id=1, source_target_pairs={{24,0},{16,8},{8,16},{0,24},{25,1},{17,9},{9,17},{1,25},{26,2},{18... | collective-permute-start | bytes 12296 | tf_op jit(solution)/shard_map/ppermute | solution.py:26
  10.5 5.7 %collective-permute-start.4 = (bf16[16,128]{1,0:T(8,128)(2,1)}, bf16[16,128]{1,0:T(8,128)(2,1)S(1)}, u32[]{:S(2)}, u32[]{:S(2)}) collective-permute-start(bf16[16,128]{1,0:T(8,128)(2,1)} %param.8), channel_id=1, source_target_pairs={{16,0},{24,8},{0,16},{8,24},{17,1},{25,9},{1,17},{9,25},{18,2},{26... | collective-permute-start | bytes 12296 | tf_op jit(solution)/shard_map/ppermute | solution.py:26
  11.1 5.1 %collective-permute-start.3 = (bf16[16,128]{1,0:T(8,128)(2,1)}, bf16[16,128]{1,0:T(8,128)(2,1)S(1)}, u32[]{:S(2)}, u32[]{:S(2)}) collective-permute-start(bf16[16,128]{1,0:T(8,128)(2,1)} %param.8), channel_id=1, source_target_pairs={{8,0},{0,8},{24,16},{16,24},{9,1},{1,9},{25,17},{17,25},{10,2},{2,... | collective-permute-start | bytes 12296 | tf_op jit(solution)/shard_map/ppermute | solution.py:26
  12.5 6.3 %collective-permute-start.2 = (bf16[384,128]{1,0:T(8,128)(2,1)S(1)}, bf16[384,128]{1,0:T(8,128)(2,1)S(1)}, u32[]{:S(2)}, u32[]{:S(2)}) collective-permute-start(bf16[384,128]{1,0:T(8,128)(2,1)S(1)} %get-tuple-element.75), channel_id=1, source_target_pairs={{24,0},{16,8},{8,16},{0,24},{25,1},{17,9},{9,17},{1,25},{26,2},{18... | collective-permute-start | bytes 294920 | tf_op jit(solution)/shard_map/ppermute | solution.py:26
  15.3 3.5 %collective-permute-start.1 = (bf16[384,128]{1,0:T(8,128)(2,1)S(1)}, bf16[384,128]{1,0:T(8,128)(2,1)S(1)}, u32[]{:S(2)}, u32[]{:S(2)}) collective-permute-start(bf16[384,128]{1,0:T(8,128)(2,1)S(1)} %get-tuple-element.73), channel_id=1, source_target_pairs={{8,0},{0,8},{24,16},{16,24},{9,1},{1,9},{25,17},{17,25},{10,2},{2,... | collective-permute-start | bytes 294920 | tf_op jit(solution)/shard_map/ppermute | solution.py:26
  15.7 6.3 %collective-permute-start = (bf16[384,128]{1,0:T(8,128)(2,1)S(1)}, bf16[384,128]{1,0:T(8,128)(2,1)S(1)}, u32[]{:S(2)}, u32[]{:S(2)}) collective-permute-start(bf16[384,128]{1,0:T(8,128)(2,1)S(1)} %get-tuple-element.74), channel_id=1, source_target_pairs={{16,0},{24,8},{0,16},{8,24},{17,1},{25,9},{1,17},{9,25},{18,2},{26... | collective-permute-start | bytes 294920 | tf_op jit(solution)/shard_map/ppermute | solution.py:26
  22.0 10.4 %collective-permute-start.6 = (bf16[1536,128]{1,0:T(8,128)(2,1)S(1)}, bf16[1536,128]{1,0:T(8,128)(2,1)S(1)}, u32[]{:S(2)}, u32[]{:S(2)}) collective-permute-start(bf16[1536,128]{1,0:T(8,128)(2,1)S(1)} %pad_maximum_fusion.4), channel_id=1, source_target_pairs={{0,4},{4,0},{1,5},{5,1},{2,6},{6,2},{3,7},{7,3},{8,12},{12,8},{9,1... | collective-permute-start | bytes 1179656 | tf_op jit(solution)/shard_map/ppermute | solution.py:18
  32.5 40.5 %copy-start.3 = (bf16[1536,256]{1,0:T(8,128)(2,1)}, bf16[1536,256]{1,0:T(8,128)(2,1)S(1)}, u32[]{:S(2)}) copy-start(bf16[1536,256]{1,0:T(8,128)(2,1)S(1)} %pad_maximum_fusion.3) | copy-start | bytes 2359300
  32.5 44.0 %collective-permute-start.7 = (bf16[384,1848]{0,1:T(8,128)(2,1)S(1)}, bf16[384,1848]{0,1:T(8,128)(2,1)S(1)}, u32[]{:S(2)}, u32[]{:S(2)}) collective-permute-start(bf16[384,1848]{0,1:T(8,128)(2,1)S(1)} %copy-done.2), channel_id=1, source_target_pairs={{0,16},{16,0},{1,17},{17,1},{2,18},{18,2},{3,19},{19,3},{4,20},{20... | collective-permute-start | bytes 4257800 | tf_op jit(solution)/shard_map/ppermute | solution.py:18
  35.4 26.7 %collective-permute-start.11 = (bf16[1536,256]{1,0:T(8,128)(2,1)S(1)}, bf16[1536,256]{1,0:T(8,128)(2,1)S(1)}, u32[]{:S(2)}, u32[]{:S(2)}) collective-permute-start(bf16[1536,256]{1,0:T(8,128)(2,1)S(1)} %pad_maximum_fusion.3), channel_id=1, source_target_pairs={{1,0},{0,1},{3,2},{2,3},{5,4},{4,5},{7,6},{6,7},{9,8},{8,9},{11,10... | collective-permute-start | bytes 2359304 | tf_op jit(solution)/shard_map/ppermute | solution.py:26
  37.0 36.1 %collective-permute-start.12 = (bf16[1536,256]{1,0:T(8,128)(2,1)S(1)}, bf16[1536,256]{1,0:T(8,128)(2,1)S(1)}, u32[]{:S(2)}, u32[]{:S(2)}) collective-permute-start(bf16[1536,256]{1,0:T(8,128)(2,1)S(1)} %pad_maximum_fusion.3), channel_id=1, source_target_pairs={{2,0},{3,1},{0,2},{1,3},{6,4},{7,5},{4,6},{5,7},{10,8},{11,9},{8,1... | collective-permute-start | bytes 2359304 | tf_op jit(solution)/shard_map/ppermute | solution.py:26
  39.9 35.7 %collective-permute-start.13 = (bf16[1536,256]{1,0:T(8,128)(2,1)S(1)}, bf16[1536,256]{1,0:T(8,128)(2,1)S(1)}, u32[]{:S(2)}, u32[]{:S(2)}) collective-permute-start(bf16[1536,256]{1,0:T(8,128)(2,1)S(1)} %pad_maximum_fusion.3), channel_id=1, source_target_pairs={{3,0},{2,1},{1,2},{0,3},{7,4},{6,5},{5,6},{4,7},{11,8},{10,9},{9,1... | collective-permute-start | bytes 2359304 | tf_op jit(solution)/shard_map/ppermute | solution.py:26
  40.1 5.1 %collective-permute-start.8 = (bf16[1,16,512]{2,1,0:T(8,128)(2,1)S(1)}, bf16[1,16,512]{2,1,0:T(8,128)(2,1)S(1)}, u32[]{:S(2)}, u32[]{:S(2)}) collective-permute-start(bf16[1,16,512]{2,1,0:T(8,128)(2,1)S(1)} %maximum_bitcast_fusion), channel_id=1, source_target_pairs={{32,0},{64,32},{96,64},{128,96},{160,128},{192,160},{224,192},{0,2... | collective-permute-start | bytes 49160 | tf_op jit(solution)/shard_map/ppermute | solution.py:22
  45.2 7.0 %collective-permute-start.9 = (bf16[2,16,512]{2,1,0:T(8,128)(2,1)S(1)}, bf16[2,16,512]{2,1,0:T(8,128)(2,1)S(1)}, u32[]{:S(2)}, u32[]{:S(2)}) collective-permute-start(bf16[2,16,512]{2,1,0:T(8,128)(2,1)S(1)} %pad_maximum_fusion.12), channel_id=1, source_target_pairs={{64,0},{96,32},{128,64},{160,96},{192,128},{224,160},{0,192},{32,2... | collective-permute-start | bytes 98312 | tf_op jit(solution)/shard_map/ppermute | solution.py:22
  52.3 9.8 %collective-permute-start.10 = (bf16[4,16,512]{2,1,0:T(8,128)(2,1)S(1)}, bf16[4,16,512]{2,1,0:T(8,128)(2,1)S(1)}, u32[]{:S(2)}, u32[]{:S(2)}) collective-permute-start(bf16[4,16,512]{2,1,0:T(8,128)(2,1)S(1)} %pad_maximum_fusion.9), channel_id=1, source_target_pairs={{128,0},{160,32},{192,64},{224,96},{0,128},{32,160},{64,192},{96,2... | collective-permute-start | bytes 196616 | tf_op jit(solution)/shard_map/ppermute | solution.py:22
  62.2 13.5 %copy-start.6 = (bf16[1536,256]{1,0:T(8,128)(2,1)}, bf16[1536,256]{1,0:T(8,128)(2,1)S(1)}, u32[]{:S(2)}) copy-start(bf16[1536,256]{1,0:T(8,128)(2,1)S(1)} %collective-permute-done.11) | copy-start | bytes 2359300
  73.1 2.6 %copy-start.7 = (bf16[1536,256]{1,0:T(8,128)(2,1)}, bf16[1536,256]{1,0:T(8,128)(2,1)S(1)}, u32[]{:S(2)}) copy-start(bf16[1536,256]{1,0:T(8,128)(2,1)S(1)} %collective-permute-done.12) | copy-start | bytes 2359300
  75.6 0.9 copy-start.8
  78.3 14.8 %collective-permute-start.17 = (bf16[768,1848]{0,1:T(8,128)(2,1)}, bf16[768,1848]{0,1:T(8,128)(2,1)}, u32[]{:S(2)}, u32[]{:S(2)}) collective-permute-start(bf16[768,1848]{0,1:T(8,128)(2,1)} %pad_maximum_fusion.2), channel_id=1, source_target_pairs={{0,8},{8,0},{1,9},{9,1},{2,10},{10,2},{3,11},{11,3},{4,12},{12,4},... | collective-permute-start | bytes 8515592 | tf_op jit(solution)/shard_map/ppermute | solution.py:18
  78.8 4.2 %collective-permute-start.14 = (f32[32,384]{1,0:T(8,128)S(1)}, f32[32,384]{1,0:T(8,128)S(1)}, u32[]{:S(2)}, u32[]{:S(2)}) collective-permute-start(f32[32,384]{1,0:T(8,128)S(1)} %pad_maximum_fusion.10), channel_id=1, source_target_pairs={{1,0},{0,1},{3,2},{2,3},{5,4},{4,5},{7,6},{6,7},{9,8},{8,9},{11,10... | collective-permute-start | bytes 147464 | tf_op jit(solution)/shard_map/ppermute | solution.py:26
  83.1 5.7 %collective-permute-start.15 = (f32[32,384]{1,0:T(8,128)S(1)}, f32[32,384]{1,0:T(8,128)S(1)}, u32[]{:S(2)}, u32[]{:S(2)}) collective-permute-start(f32[32,384]{1,0:T(8,128)S(1)} %fusion.29), channel_id=1, source_target_pairs={{2,0},{3,1},{0,2},{1,3},{6,4},{7,5},{4,6},{5,7},{10,8},{11,9},{8,1... | collective-permute-start | bytes 147464 | tf_op jit(solution)/shard_map/ppermute | solution.py:26
  88.7 4.4 %collective-permute-start.16 = (f32[32,384]{1,0:T(8,128)S(1)}, f32[32,384]{1,0:T(8,128)S(1)}, u32[]{:S(2)}, u32[]{:S(2)}) collective-permute-start(f32[32,384]{1,0:T(8,128)S(1)} %add.128), channel_id=1, source_target_pairs={{4,0},{5,1},{6,2},{7,3},{0,4},{1,5},{2,6},{3,7},{12,8},{13,9},{14,... | collective-permute-start | bytes 147464 | tf_op jit(solution)/shard_map/ppermute | solution.py:26
  97.8 2.1 %copy-start.1 = (bf16[1848,1024]{1,0:T(8,128)(2,1)S(1)}, bf16[1848,1024]{1,0:T(8,128)(2,1)}, u32[]{:S(2)}) copy-start(bf16[1848,1024]{1,0:T(8,128)(2,1)} %all-gather.2.cloned.1.call-done.in_ref) | copy-start | bytes 11354116
  99.9 3.0 %copy-start.4 = (bf16[1536,1024]{1,0:T(8,128)(2,1)S(1)}, bf16[1536,1024]{1,0:T(8,128)(2,1)}, u32[]{:S(2)}) copy-start(bf16[1536,1024]{1,0:T(8,128)(2,1)} %pad_maximum_fusion.1) | copy-start | bytes 9437188
  99.9 8.1 %slice-start = ((s8[5677056]{0:T(1024)(128)(4,1)}), s8[4194304]{0:T(1024)(128)(4,1)S(1)}, s32[]{:S(2)}) async-start(s8[5677056]{0:T(1024)(128)(4,1)} %bitcast.26), calls=%async_computation.1 | async-start | bytes 8388608
  102.9 5.1 %slice-start.1 = ((s8[5677056]{0:T(1024)(128)(4,1)}), s8[1482752]{0:T(1024)(128)(4,1)S(1)}, s32[]{:S(2)}) async-start(s8[5677056]{0:T(1024)(128)(4,1)} %bitcast.26), calls=%async_computation.2 | async-start | bytes 2965504
  106.3 7.0 %collective-permute-start.18 = (bf16[768,1848]{0,1:T(8,128)(2,1)S(1)}, bf16[768,1848]{0,1:T(8,128)(2,1)S(1)}, u32[]{:S(2)}, u32[]{:S(2)}) collective-permute-start(bf16[768,1848]{0,1:T(8,128)(2,1)S(1)} %convolution_convert_fusion), channel_id=1, source_target_pairs={{0,8},{8,0},{1,9},{9,1},{2,10},{10,2},{3,11},{11,3},{4,12},{12,4},... | collective-permute-start | bytes 8515592 | tf_op jit(solution)/shard_map/ppermute | solution.py:18
  106.4 5.6 %collective-permute-start.19 = (bf16[16,384]{1,0:T(8,128)(2,1)S(1)}, bf16[16,384]{1,0:T(8,128)(2,1)S(1)}, u32[]{:S(2)}, u32[]{:S(2)}) collective-permute-start(bf16[16,384]{1,0:T(8,128)(2,1)S(1)} %slice.64), channel_id=1, source_target_pairs={{0,16},{16,0},{1,17},{17,1},{2,18},{18,2},{3,19},{19,3},{4,20},{20... | collective-permute-start | bytes 36872 | tf_op jit(solution)/shard_map/ppermute | solution.py:18
  109.9 1.9 copy-start.5
  112.0 1.3 collective-permute-start.20
  112.3 6.1 %collective-permute-start.22 = (f32[16,2360]{1,0:T(8,128)S(1)}, f32[16,2360]{1,0:T(8,128)S(1)}, u32[]{:S(2)}, u32[]{:S(2)}) collective-permute-start(f32[16,2360]{1,0:T(8,128)S(1)} %pad_maximum_fusion.7), channel_id=1, source_target_pairs={{0,8},{8,0},{1,9},{9,1},{2,10},{10,2},{3,11},{11,3},{4,12},{12,4},... | collective-permute-start | bytes 453128 | tf_op jit(solution)/shard_map/ppermute | solution.py:18
  115.5 35.0 %collective-permute-start.21 = (bf16[384,1848]{0,1:T(8,128)(2,1)S(1)}, bf16[384,1848]{0,1:T(8,128)(2,1)S(1)}, u32[]{:S(2)}, u32[]{:S(2)}) collective-permute-start(bf16[384,1848]{0,1:T(8,128)(2,1)S(1)} %fusion.1), channel_id=1, source_target_pairs={{0,16},{16,0},{1,17},{17,1},{2,18},{18,2},{3,19},{19,3},{4,20},{20... | collective-permute-start | bytes 4257800 | tf_op jit(solution)/shard_map/ppermute | solution.py:18
  120.4 33.2 %collective-permute-start.25 = (bf16[1536,256]{1,0:T(8,128)(2,1)S(1)}, bf16[1536,256]{1,0:T(8,128)(2,1)S(1)}, u32[]{:S(2)}, u32[]{:S(2)}) collective-permute-start(bf16[1536,256]{1,0:T(8,128)(2,1)S(1)} %convolution_convert_fusion.1), channel_id=1, source_target_pairs={{2,0},{3,1},{0,2},{1,3},{6,4},{7,5},{4,6},{5,7},{10,8},{11,9},{8,1... | collective-permute-start | bytes 2359304 | tf_op jit(solution)/shard_map/ppermute | solution.py:26
  120.5 37.5 %collective-permute-start.24 = (bf16[1536,256]{1,0:T(8,128)(2,1)S(1)}, bf16[1536,256]{1,0:T(8,128)(2,1)S(1)}, u32[]{:S(2)}, u32[]{:S(2)}) collective-permute-start(bf16[1536,256]{1,0:T(8,128)(2,1)S(1)} %convolution_convert_fusion.3), channel_id=1, source_target_pairs={{3,0},{2,1},{1,2},{0,3},{7,4},{6,5},{5,6},{4,7},{11,8},{10,9},{9,1... | collective-permute-start | bytes 2359304 | tf_op jit(solution)/shard_map/ppermute | solution.py:26
  123.4 34.5 %collective-permute-start.23 = (bf16[1536,256]{1,0:T(8,128)(2,1)S(1)}, bf16[1536,256]{1,0:T(8,128)(2,1)S(1)}, u32[]{:S(2)}, u32[]{:S(2)}) collective-permute-start(bf16[1536,256]{1,0:T(8,128)(2,1)S(1)} %convolution_convert_fusion.4), channel_id=1, source_target_pairs={{1,0},{0,1},{3,2},{2,3},{5,4},{4,5},{7,6},{6,7},{9,8},{8,9},{11,10... | collective-permute-start | bytes 2359304 | tf_op jit(solution)/shard_map/ppermute | solution.py:26
  158.4 10.9 %collective-permute-start.26 = (bf16[1536,128]{1,0:T(8,128)(2,1)S(1)}, bf16[1536,128]{1,0:T(8,128)(2,1)S(1)}, u32[]{:S(2)}, u32[]{:S(2)}) collective-permute-start(bf16[1536,128]{1,0:T(8,128)(2,1)S(1)} %slice.130), channel_id=1, source_target_pairs={{0,4},{4,0},{1,5},{5,1},{2,6},{6,2},{3,7},{7,3},{8,12},{12,8},{9,1... | collective-permute-start | bytes 1179656 | tf_op jit(solution)/shard_map/ppermute | solution.py:18
  159.7 5.5 %collective-permute-start.29 = (f32[16,2360]{1,0:T(8,128)S(1)}, f32[16,2360]{1,0:T(8,128)S(1)}, u32[]{:S(2)}, u32[]{:S(2)}) collective-permute-start(f32[16,2360]{1,0:T(8,128)S(1)} %fusion.30), channel_id=1, source_target_pairs={{32,0},{0,32},{96,64},{64,96},{160,128},{128,160},{224,192},{192,2... | collective-permute-start | bytes 453128 | tf_op jit(solution)/shard_map/ppermute | solution.py:26
  165.2 8.9 %collective-permute-start.30 = (f32[16,2360]{1,0:T(8,128)S(1)}, f32[16,2360]{1,0:T(8,128)S(1)}, u32[]{:S(2)}, u32[]{:S(2)}) collective-permute-start(f32[16,2360]{1,0:T(8,128)S(1)} %add.147), channel_id=1, source_target_pairs={{64,0},{96,32},{0,64},{32,96},{192,128},{224,160},{128,192},{160,2... | collective-permute-start | bytes 453128 | tf_op jit(solution)/shard_map/ppermute | solution.py:26
  169.6 18.7 %collective-permute-start.27 = (bf16[768,128]{1,0:T(8,128)(2,1)S(1)}, bf16[768,128]{1,0:T(8,128)(2,1)S(1)}, u32[]{:S(2)}, u32[]{:S(2)}) collective-permute-start(bf16[768,128]{1,0:T(8,128)(2,1)S(1)} %get-tuple-element.70), channel_id=1, source_target_pairs={{0,8},{8,0},{1,9},{9,1},{2,10},{10,2},{3,11},{11,3},{4,12},{12,4},... | collective-permute-start | bytes 589832 | tf_op jit(solution)/shard_map/ppermute | solution.py:18
  174.1 12.9 %collective-permute-start.31 = (f32[16,2360]{1,0:T(8,128)S(1)}, f32[16,2360]{1,0:T(8,128)S(1)}, u32[]{:S(2)}, u32[]{:S(2)}) collective-permute-start(f32[16,2360]{1,0:T(8,128)S(1)} %add.148), channel_id=1, source_target_pairs={{128,0},{160,32},{192,64},{224,96},{0,128},{32,160},{64,192},{96,2... | collective-permute-start | bytes 453128 | tf_op jit(solution)/shard_map/ppermute | solution.py:26
  187.0 8.6 %collective-permute-start.32 = (f32[16,2360]{1,0:T(8,128)S(1)}, f32[16,2360]{1,0:T(8,128)S(1)}, u32[]{:S(2)}, u32[]{:S(2)}) collective-permute-start(f32[16,2360]{1,0:T(8,128)S(1)} %add.149), channel_id=1, source_target_pairs={{0,16},{16,0},{1,17},{17,1},{2,18},{18,2},{3,19},{19,3},{4,20},{20... | collective-permute-start | bytes 453128 | tf_op jit(solution)/shard_map/ppermute | solution.py:18
  188.4 9.6 %collective-permute-start.28 = (bf16[384,256]{1,0:T(8,128)(2,1)S(1)}, bf16[384,256]{1,0:T(8,128)(2,1)S(1)}, u32[]{:S(2)}, u32[]{:S(2)}) collective-permute-start(bf16[384,256]{1,0:T(8,128)(2,1)S(1)} %get-tuple-element.68), channel_id=1, source_target_pairs={{0,16},{16,0},{1,17},{17,1},{2,18},{18,2},{3,19},{19,3},{4,20},{20... | collective-permute-start | bytes 589832 | tf_op jit(solution)/shard_map/ppermute | solution.py:18
Sparse Core Ops, SparseCore 0:
  9.7 65.3 all-gather.1
where the time goes:
time: 206 us
  waiting for transfers between devices  113 us (55%)
  starting transfers between devices  38.7 us (19%)
  matrix products  17.6 us (9%)
  between operations  14.4 us (7%)
  other arithmetic  13.7 us (7%)
  local copies, waits for them, and re-layouts  5.61 us (3%)
  Pallas kernels  3.01 us (1%)
    ppermute x18, waiting for transfers between devices, from_xor(): return lax.ppermute(x, axis, [(i ^ k, i) for i in range(n)])  50.9 us
    ppermute x12, waiting for transfers between devices, swap(): return lax.ppermute(x, axis, [(0, 1), (1, 0)])  43.2 us
    ppermute x18, starting transfers between devices, from_xor(): return lax.ppermute(x, axis, [(i ^ k, i) for i in range(n)])  21.1 us
    ppermute x3, waiting for transfers between devices, from_offset(): return lax.ppermute(x, 'z', [((i + k) % NZ, i) for i in range(NZ)])  18 us
    dot_general x13, matrix products, dot(): lax.dot_general(a, b, (((ca,), (cb,)), ((), ())), preferred_element_type=...  17.6 us
    ppermute x12, starting transfers between devices, swap(): return lax.ppermute(x, axis, [(0, 1), (1, 0)])  13.5 us
    concatenate x1, other arithmetic, local(): all_hidden = jnp.concatenate([hidden_x, swap(hidden_x, 'core')], 0)  4.67 us
  transfers between devices with their start and end apart: 34, of which 20 were waited for; matrix products, arithmetic and copies ran while one was open for 14% of the time, Pallas kernels for 0%

commit v1 on v0

--- a/solution.py
+++ b/solution.py
@@ -84,26 +84,32 @@
     mine = jnp.concatenate(mine, 0)
     g = jnp.concatenate(g, 1)[None]
     mine, g = together((mine, g))
-    cot_t, hidden_own = together((jnp.concatenate([mine, swap(mine, "x_lo")], 1), hidden))
+    swapped = swap(mine, "x_lo")
+    near = [from_xor(mine, "y", NY, k) for k in (1, 3)]
+    swapped, near, mine, hidden_own = together((swapped, near, mine, hidden))
     hidden_x = swap(hidden_own, "x_hi")
-    cots = [cot_t] + [from_xor(cot_t, "y", NY, k) for k in range(1, NY)]
+    far = from_xor(jnp.concatenate([mine, swapped], 1), "y", NY, 2)
+    others = [from_xor(swapped, "y", NY, k) for k in (1, 3)]
+    cots = [mine, swapped, near[0], others[0], far, near[1], others[1]]
     for k in (1, 2, 4):
         g = jnp.concatenate([g, from_offset(g, k)], 0)
     hidden_x, g, cots = together((hidden_x, g, cots))
+
     hidden_x = jnp.concatenate([hidden, hidden_x], 0)
-    all_hidden = jnp.concatenate([hidden_x, swap(hidden_x, "core")], 0)
-    cots = jnp.concatenate(cots, 1)
-
+    hidden_c = swap(hidden_x, "core")
     cot_rel = jnp.concatenate(cot_g, 1)
     factor = lax.dynamic_index_in_dim(g, (t - z) % NZ, 0, keepdims=False)
     x = jnp.concatenate([dot(a_in, hidden, 1, 1), dot(factor, cot_rel, 1, 1)], 0)
-    for k in (1, 2, 4):
-        x = x + from_xor(x, TENSOR, NT, k)
+    x = x + from_xor(x, TENSOR, NT, 1)
+    x, cots = together((x, jnp.concatenate(cots, 1)))
+    x = x + from_xor(x, TENSOR, NT, 2)
+    at = [(x_lo ^ i) * NY + (y ^ k) for k in range(NY) for i in range(2)]
+    x, all_w = together((x, reorder(all_w, jnp.stack(at))))
+    x = x + from_xor(x, TENSOR, NT, 4)
+    x, all_hidden = together((x, jnp.concatenate([hidden_x, hidden_c], 0)))
     ranks = x.astype(BF16)
 
-    cots, all_w, ranks, all_hidden = together((cots, all_w, ranks, all_hidden))
-    at = [(x_lo ^ i) * NY + (y ^ k) for k in range(NY) for i in range(2)]
-    all_w = reorder(all_w, jnp.stack(at))
+    cots, all_w, all_hidden = together((cots, all_w, all_hidden))
 
     def forward(k):
         return dot(all_hidden, all_w[:, 2 * k * group : 2 * (k + 1) * group], 1, 0).astype(BF16)
@@ -118,6 +124,7 @@
     c = SCALE / math.sqrt(tokens * 32)
     grads = jnp.concatenate([c * dot(back, hidden, 1, 0), c * dot(rank, cot, 1, 0)], 1)
     grads = grads + swap(grads, "core")
+    all_grads = lax.all_gather(grads, "z", axis=0)
     rank_x = jnp.concatenate([rank, swap(rank, "x_hi")], 1)
     all_rank = jnp.concatenate([rank_x, swap(rank_x, "core")], 1)
     got, shares, cots, all_hidden, all_rank = together((got, shares, cots, all_hidden, all_rank))
@@ -125,23 +132,22 @@
     give = (backward(1, 2) + got[tokens:].astype(F32)).astype(BF16)
     give, all_hidden = together((give, all_hidden))
     last = swap(give, "x_hi")
-    shares = {2: forward(2), 0: forward(0)}
+    shares = together({2: forward(2), 0: forward(0)})
     sent[2] = from_xor(shares[2], "y", NY, 2)
-    cots, main, last, grads = together((cots, shares[0], last, grads))
-    own = backward(0, 1) + got[:tokens].astype(F32) + SCALE * dot(back, a_in, 0, 0)
-    for k in (1, 2, 4):
-        grads = grads + from_xor(grads, "z", NZ, k)
+    main, last, sent[1], sent[3], cots = together((shares[0], last, sent[1], sent[3], cots))
+    grads = jnp.sum(all_grads, 0)
     grads = grads + swap(grads, "x_hi")
-    main, own = together((main, own))
 
     main = main.astype(F32)
     for k in (1, 3, 2):
         main = main + sent[k].astype(F32)
     main = main[:, :group] + swap(main[:, group:].astype(BF16), "x_lo").astype(F32)
     out = (main + SCALE * dot(all_rank, factor[:, :group], 0, 0)).astype(BF16)
-    out = jnp.concatenate([out[: 2 * tokens], swap(out[2 * tokens :], "core")], 1)
-    out = jnp.concatenate([out[:tokens], swap(out[tokens:], "x_hi")], 1)
-    projected = jnp.concatenate(groups(out, x_hi, core), 1)
+    rows = {0: 0, 2: 1, 1: 2, 3: 3}
+    out = {k: out[i * tokens : (i + 1) * tokens] for k, i in rows.items()}
+    out = [out[0]] + [from_quad(out[k], k) for k in range(1, 4)]
+    projected = jnp.concatenate(groups(jnp.concatenate(out, 1), x_hi, core), 1)
+    own = backward(0, 1) + got[:tokens].astype(F32) + SCALE * dot(back, a_in, 0, 0)
     hidden_gradient = (own + last.astype(F32)).astype(BF16)
     return projected, hidden_gradient, grads[:, :units], grads[:, units:]
 

time: 206 us -> 189 us (0.917)
  the two profiles are of different devices: /device:TPU:96 before, /device:TPU:1 now
where the time goes in v1:
time: 189 us; the launch traced here: 188 us
  waiting for transfers between devices  67.4 us (36%)
  starting transfers between devices  52.4 us (28%)
  matrix products  29.9 us (16%)
  between operations  14.5 us (8%)
  other arithmetic  11.8 us (6%)
  local copies, waits for them, and re-layouts  9.47 us (5%)
  Pallas kernels  2.98 us (2%)
    dot_general x13, matrix products, dot(): lax.dot_general(a, b, (((ca,), (cb,)), ((), ())), preferred_element_type=...  29.9 us
    ppermute x20, starting transfers between devices, from_xor(): return lax.ppermute(x, axis, [(i ^ k, i) for i in range(n)])  28.7 us
    ppermute x20, waiting for transfers between devices, from_xor(): return lax.ppermute(x, axis, [(i ^ k, i) for i in range(n)])  22.8 us
    all_gather x1, waiting for transfers between devices, local(): all_grads = lax.all_gather(grads, 'z', axis=0)  19.6 us
    ppermute x10, waiting for transfers between devices, swap(): return lax.ppermute(x, axis, [(0, 1), (1, 0)])  16.9 us
    ppermute x10, starting transfers between devices, swap(): return lax.ppermute(x, axis, [(0, 1), (1, 0)])  13.4 us
    ppermute x3, starting transfers between devices, from_offset(): return lax.ppermute(x, 'z', [((i + k) % NZ, i) for i in range(NZ)])  10.2 us
    ppermute x3, waiting for transfers between devices, from_offset(): return lax.ppermute(x, 'z', [((i + k) % NZ, i) for i in range(NZ)])  7.42 us
  transfers between devices with their start and end apart: 35, of which 18 were waited for; matrix products, arithmetic and copies ran while one was open for 20% of the time, Pallas kernels for 2%

profile of v1, /device:TPU:1, one launch (start us, length us, event | category | flops | bytes accessed | tf_op | source)
XLA Modules:
  0.0 188.4 jit_solution(6951494289105083493)
XLA Ops:
  7.2 0.7 all-gather.4.cloned.1.call-update
  8.0 4.2 %collective-permute-start.5 = (bf16[16,128]{1,0:T(8,128)(2,1)}, bf16[16,128]{1,0:T(8,128)(2,1)S(1)}, u32[]{:S(2)}, u32[]{:S(2)}) collective-permute-start(bf16[16,128]{1,0:T(8,128)(2,1)} %param.8), channel_id=1, source_target_pairs={{24,0},{16,8},{8,16},{0,24},{25,1},{17,9},{9,17},{1,25},{26,2},{18... | collective-permute-start | bytes 12296 | tf_op jit(solution)/shard_map/ppermute | solution.py:26
  12.2 2.0 %collective-permute-start.4 = (bf16[16,128]{1,0:T(8,128)(2,1)}, bf16[16,128]{1,0:T(8,128)(2,1)S(1)}, u32[]{:S(2)}, u32[]{:S(2)}) collective-permute-start(bf16[16,128]{1,0:T(8,128)(2,1)} %param.8), channel_id=1, source_target_pairs={{16,0},{24,8},{0,16},{8,24},{17,1},{25,9},{1,17},{9,25},{18,2},{26... | collective-permute-start | bytes 12296 | tf_op jit(solution)/shard_map/ppermute | solution.py:26
  14.2 1.7 constant_dynamic-slice_fusion.7
  15.9 1.4 collective-permute-start.2
  17.4 1.9 collective-permute-start
  19.3 0.7 maximum_bitcast_fusion
  20.0 2.5 %collective-permute-done.2 = bf16[384,128]{1,0:T(8,128)(2,1)S(1)} collective-permute-done((bf16[384,128]{1,0:T(8,128)(2,1)S(1)}, bf16[384,128]{1,0:T(8,128)(2,1)S(1)}, u32[]{:S(2)}, u32[]{:S(2)}) %collective-permute-start.2) | collective-permute-done | bytes 98336 | tf_op jit(solution)/shard_map/ppermute | solution.py:26
  22.5 2.0 %collective-permute-done = bf16[384,128]{1,0:T(8,128)(2,1)S(1)} collective-permute-done((bf16[384,128]{1,0:T(8,128)(2,1)}, bf16[384,128]{1,0:T(8,128)(2,1)S(1)}, u32[]{:S(2)}, u32[]{:S(2)}) %collective-permute-start) | collective-permute-done | bytes 98336 | tf_op jit(solution)/shard_map/ppermute | solution.py:26
  24.8 1.9 %collective-permute-start.8 = (bf16[1536,128]{1,0:T(8,128)(2,1)S(1)}, bf16[1536,128]{1,0:T(8,128)(2,1)S(1)}, u32[]{:S(2)}, u32[]{:S(2)}) collective-permute-start(bf16[1536,128]{1,0:T(8,128)(2,1)S(1)} %pad_maximum_fusion.3), channel_id=1, source_target_pairs={{3,0},{2,1},{1,2},{0,3},{7,4},{6,5},{5,6},{4,7},{11,8},{10,9},{9,1... | collective-permute-start | bytes 1179656 | tf_op jit(solution)/shard_map/ppermute | solution.py:26
  26.7 8.0 %collective-permute-done.6 = bf16[1536,128]{1,0:T(8,128)(2,1)S(1)} collective-permute-done((bf16[1536,128]{1,0:T(8,128)(2,1)S(1)}, bf16[1536,128]{1,0:T(8,128)(2,1)S(1)}, u32[]{:S(2)}, u32[]{:S(2)}) %collective-permute-start.6) | collective-permute-done | bytes 393248 | tf_op jit(solution)/shard_map/ppermute | solution.py:18
  34.9 0.7 copy-done.14
  35.6 0.8 copy-done.12
  36.4 2.7 %collective-permute-start.9 = (bf16[384,1848]{0,1:T(8,128)(2,1)}, bf16[384,1848]{0,1:T(8,128)(2,1)S(1)}, u32[]{:S(2)}, u32[]{:S(2)}) collective-permute-start(bf16[384,1848]{0,1:T(8,128)(2,1)} %param.5), channel_id=1, source_target_pairs={{0,16},{16,0},{1,17},{17,1},{2,18},{18,2},{3,19},{19,3},{4,20},{20... | collective-permute-start | bytes 4257800 | tf_op jit(solution)/shard_map/ppermute | solution.py:18
  39.2 1.6 collective-permute-start.14
  40.8 5.6 %collective-permute-start.10 = (bf16[1,16,512]{2,1,0:T(8,128)(2,1)S(1)}, bf16[1,16,512]{2,1,0:T(8,128)(2,1)S(1)}, u32[]{:S(2)}, u32[]{:S(2)}) collective-permute-start(bf16[1,16,512]{2,1,0:T(8,128)(2,1)S(1)} %maximum_bitcast_fusion), channel_id=1, source_target_pairs={{32,0},{64,32},{96,64},{128,96},{160,128},{192,160},{224,192},{0,2... | collective-permute-start | bytes 49160 | tf_op jit(solution)/shard_map/ppermute | solution.py:22
  46.4 1.0 collective-permute-start.13
  47.5 0.8 collective-permute-start.15
  48.3 1.8 collective-permute-start.11
  50.0 2.9 %collective-permute-done.11 = bf16[2,16,512]{2,1,0:T(8,128)(2,1)S(1)} collective-permute-done((bf16[2,16,512]{2,1,0:T(8,128)(2,1)S(1)}, bf16[2,16,512]{2,1,0:T(8,128)(2,1)S(1)}, u32[]{:S(2)}, u32[]{:S(2)}) %collective-permute-start.11) | collective-permute-done | bytes 32800 | tf_op jit(solution)/shard_map/ppermute | solution.py:22
  53.0 2.9 %collective-permute-start.12 = (bf16[4,16,512]{2,1,0:T(8,128)(2,1)S(1)}, bf16[4,16,512]{2,1,0:T(8,128)(2,1)S(1)}, u32[]{:S(2)}, u32[]{:S(2)}) collective-permute-start(bf16[4,16,512]{2,1,0:T(8,128)(2,1)S(1)} %pad_maximum_fusion.8), channel_id=1, source_target_pairs={{128,0},{160,32},{192,64},{224,96},{0,128},{32,160},{64,192},{96,2... | collective-permute-start | bytes 196616 | tf_op jit(solution)/shard_map/ppermute | solution.py:22
  55.8 4.5 %collective-permute-done.12 = bf16[4,16,512]{2,1,0:T(8,128)(2,1)S(1)} collective-permute-done((bf16[4,16,512]{2,1,0:T(8,128)(2,1)S(1)}, bf16[4,16,512]{2,1,0:T(8,128)(2,1)S(1)}, u32[]{:S(2)}, u32[]{:S(2)}) %collective-permute-start.12) | collective-permute-done | bytes 65568 | tf_op jit(solution)/shard_map/ppermute | solution.py:22
  60.3 5.0 %collective-permute-done.13 = bf16[1536,128]{1,0:T(8,128)(2,1)S(1)} collective-permute-done((bf16[1536,128]{1,0:T(8,128)(2,1)S(1)}, bf16[1536,128]{1,0:T(8,128)(2,1)S(1)}, u32[]{:S(2)}, u32[]{:S(2)}) %collective-permute-start.13) | collective-permute-done | bytes 393248 | tf_op jit(solution)/shard_map/ppermute | solution.py:26
  65.4 3.4 %collective-permute-done.15 = bf16[1536,128]{1,0:T(8,128)(2,1)S(1)} collective-permute-done((bf16[1536,128]{1,0:T(8,128)(2,1)S(1)}, bf16[1536,128]{1,0:T(8,128)(2,1)S(1)}, u32[]{:S(2)}, u32[]{:S(2)}) %collective-permute-start.15) | collective-permute-done | bytes 393248 | tf_op jit(solution)/shard_map/ppermute | solution.py:26
  68.8 0.7 copy-done.16
  69.6 0.9 copy-done.10
  70.5 1.9 %pad_maximum_fusion.1 = bf16[768,1848]{0,1:T(8,128)(2,1)} fusion(bf16[384,1848]{0,1:T(8,128)(2,1)S(1)} %collective-permute-done.9, bf16[384,1848]{0,1:T(8,128)(2,1)S(1)} %copy-done.5), kind=kLoop, calls=%fused_computation.6 | loop fusion | flops 5677056 | bytes 5677056 | tf_op jit(solution)/shard_map/concatenate | solution.py:98
  72.3 1.2 collective-permute-start.19
  73.9 1.4 fusion.11
  76.8 2.1 %collective-permute-done.16 = f32[32,384]{1,0:T(8,128)S(1)} collective-permute-done((f32[32,384]{1,0:T(8,128)S(1)}, f32[32,384]{1,0:T(8,128)S(1)}, u32[]{:S(2)}, u32[]{:S(2)}) %collective-permute-start.16) | collective-permute-done | bytes 49184 | tf_op jit(solution)/shard_map/ppermute | solution.py:26
  78.9 2.1 %collective-permute-start.17 = (f32[32,384]{1,0:T(8,128)S(1)}, f32[32,384]{1,0:T(8,128)S(1)}, u32[]{:S(2)}, u32[]{:S(2)}) collective-permute-start(f32[32,384]{1,0:T(8,128)S(1)} %fusion.24), channel_id=1, source_target_pairs={{2,0},{3,1},{0,2},{1,3},{6,4},{7,5},{4,6},{5,7},{10,8},{11,9},{8,1... | collective-permute-start | bytes 147464 | tf_op jit(solution)/shard_map/ppermute | solution.py:26
  81.1 2.4 %collective-permute-done.17 = f32[32,384]{1,0:T(8,128)S(1)} collective-permute-done((f32[32,384]{1,0:T(8,128)S(1)}, f32[32,384]{1,0:T(8,128)S(1)}, u32[]{:S(2)}, u32[]{:S(2)}) %collective-permute-start.17) | collective-permute-done | bytes 49184 | tf_op jit(solution)/shard_map/ppermute | solution.py:26
  83.5 2.1 %copy-done.1 = bf16[1848,1024]{1,0:T(8,128)(2,1)S(1)} copy-done((bf16[1848,1024]{1,0:T(8,128)(2,1)S(1)}, bf16[1848,1024]{1,0:T(8,128)(2,1)}, u32[]{:S(2)}) %copy-start.1) | copy-done | bytes 3784728
  85.5 3.0 %shard_map.84 = bf16[1848,1024]{1,0:T(8,128)(2,1)S(1)} custom-call(s32[8]{0:T(128)S(1)} %stack.35.at, bf16[1848,1024]{1,0:T(8,128)(2,1)S(1)} %copy-done.1), custom_call_target="tpu_custom_call" | custom-call | bytes 7569408 | tf_op jit(solution)/shard_map/pallas_call | solution.py:55
  88.5 1.1 collective-permute-start.18
  89.6 3.9 %pad_maximum_fusion = bf16[1536,1848]{0,1:T(8,128)(2,1)S(1)} fusion(bf16[768,1848]{0,1:T(8,128)(2,1)} %collective-permute-done.19, bf16[384,1848]{0,1:T(8,128)(2,1)S(1)} %collective-permute-done.9, bf16[384,1848]{0,1:T(8,128)(2,1)S(1)} %copy-done.5), kind=kLoop, calls=%fused_computation | loop fusion | flops 17031168 | bytes 11354112 | tf_op jit(solution)/shard_map/concatenate | solution.py:109
  93.6 4.5 %convolution_convert_fusion = bf16[768,1848]{0,1:T(8,128)(2,1)} fusion(bf16[1848,1024]{1,0:T(8,128)(2,1)S(1)} %shard_map.84, bf16[1536,1024]{1,0:T(8,128)(2,1)S(1)} %copy-done.22), kind=kOutput, calls=%fused_computation.1 | convolution fusion | flops 2908071936 | bytes 8196096 | tf_op jit(solution)/shard_map/dot_general | solution.py:30
  98.1 2.0 %collective-permute-start.20 = (bf16[768,1848]{0,1:T(8,128)(2,1)}, bf16[768,1848]{0,1:T(8,128)(2,1)}, u32[]{:S(2)}, u32[]{:S(2)}) collective-permute-start(bf16[768,1848]{0,1:T(8,128)(2,1)} %convolution_convert_fusion), channel_id=1, source_target_pairs={{0,8},{8,0},{1,9},{9,1},{2,10},{10,2},{3,11},{11,3},{4,12},{12,4},... | collective-permute-start | bytes 8515592 | tf_op jit(solution)/shard_map/ppermute | solution.py:18
  100.5 2.8 %collective-permute-start.21 = (bf16[16,384]{1,0:T(8,128)(2,1)S(1)}, bf16[16,384]{1,0:T(8,128)(2,1)S(1)}, u32[]{:S(2)}, u32[]{:S(2)}) collective-permute-start(bf16[16,384]{1,0:T(8,128)(2,1)S(1)} %slice.81), channel_id=1, source_target_pairs={{0,16},{16,0},{1,17},{17,1},{2,18},{18,2},{3,19},{19,3},{4,20},{20... | collective-permute-start | bytes 36872 | tf_op jit(solution)/shard_map/ppermute | solution.py:18
  103.3 2.8 %convolution_convert_fusion.4 = bf16[1536,256]{1,0:T(8,128)(2,1)} fusion(bf16[1536,1848]{0,1:T(8,128)(2,1)S(1)} %pad_maximum_fusion, bf16[1848,1024]{1,0:T(8,128)(2,1)S(1)} %shard_map.84), kind=kOutput, calls=%fused_computation.12 | convolution fusion | flops 1453719552 | bytes 7409664 | tf_op jit(solution)/shard_map/dot_general | solution.py:30
  106.1 2.8 %convolution_convert_fusion.3 = bf16[1536,256]{1,0:T(8,128)(2,1)} fusion(bf16[1536,1848]{0,1:T(8,128)(2,1)S(1)} %pad_maximum_fusion, bf16[1848,1024]{1,0:T(8,128)(2,1)S(1)} %shard_map.84), kind=kOutput, calls=%fused_computation.11 | convolution fusion | flops 1453719552 | bytes 7409664 | tf_op jit(solution)/shard_map/dot_general | solution.py:30
  110.4 0.8 collective-permute-done.31
  111.2 0.7 fusion.25
  112.0 6.1 %fusion.1 = bf16[384,1848]{0,1:T(8,128)(2,1)} fusion(bf16[1848,1024]{1,0:T(8,128)(2,1)} %copy-done.2, bf16[768,1848]{0,1:T(8,128)(2,1)} %collective-permute-done.20, bf16[1536,1024]{1,0:T(8,128)(2,1)} %copy-done.21), kind=kOutput, calls=%fused_computation.8 | convolution fusion | flops 1455455232 | bytes 7409664 | tf_op jit(solution)/shard_map/dot_general | solution.py:30
  118.4 2.8 %convolution_convert_fusion.2 = bf16[1536,256]{1,0:T(8,128)(2,1)} fusion(bf16[1536,1848]{0,1:T(8,128)(2,1)S(1)} %bitcast.28, bf16[1848,1024]{1,0:T(8,128)(2,1)S(1)} %copy-done.3), kind=kOutput, calls=%fused_computation.10 | convolution fusion | flops 1453719552 | bytes 7409664 | tf_op jit(solution)/shard_map/dot_general | solution.py:30
  121.4 1.5 collective-permute-start.25
  123.0 2.8 %convolution_convert_fusion.1 = bf16[1536,256]{1,0:T(8,128)(2,1)} fusion(bf16[1536,1848]{0,1:T(8,128)(2,1)S(1)} %bitcast.28, bf16[1848,1024]{1,0:T(8,128)(2,1)S(1)} %copy-done.3), kind=kOutput, calls=%fused_computation.9 | convolution fusion | flops 1453719552 | bytes 7409664 | tf_op jit(solution)/shard_map/dot_general | solution.py:30
  125.7 1.5 collective-permute-start.26
  127.2 19.6 %all-gather.6.cloned.1.call-done = f32[128,2360]{1,0:T(8,128)} async-done(((f32[16,2360]{1,0:T(8,128)}), f32[128,2360]{1,0:T(8,128)}) %all-gather.6.cloned.1.call-update) | async-done | bytes 1208336 | tf_op jit(solution)/shard_map/all_gather | solution.py:127
  146.8 1.4 reduce_sum.9
  148.1 2.6 %collective-permute-start.32 = (f32[16,2360]{1,0:T(8,128)S(1)}, f32[16,2360]{1,0:T(8,128)S(1)}, u32[]{:S(2)}, u32[]{:S(2)}) collective-permute-start(f32[16,2360]{1,0:T(8,128)S(1)} %reduce_sum.9), channel_id=1, source_target_pairs={{0,16},{16,0},{1,17},{17,1},{2,18},{18,2},{3,19},{19,3},{4,20},{20... | collective-permute-start | bytes 453128 | tf_op jit(solution)/shard_map/ppermute | solution.py:18
  150.7 3.9 %collective-permute-done.32 = f32[16,2360]{1,0:T(8,128)S(1)} collective-permute-done((f32[16,2360]{1,0:T(8,128)S(1)}, f32[16,2360]{1,0:T(8,128)S(1)}, u32[]{:S(2)}, u32[]{:S(2)}) %collective-permute-start.32) | collective-permute-done | bytes 151072 | tf_op jit(solution)/shard_map/ppermute | solution.py:18
  154.6 0.7 slice.90
  155.3 0.7 slice.91
  156.0 2.2 %collective-permute-done.26 = bf16[1536,256]{1,0:T(8,128)(2,1)S(1)} collective-permute-done((bf16[1536,256]{1,0:T(8,128)(2,1)}, bf16[1536,256]{1,0:T(8,128)(2,1)S(1)}, u32[]{:S(2)}, u32[]{:S(2)}) %collective-permute-start.26) | collective-permute-done | bytes 786464 | tf_op jit(solution)/shard_map/ppermute | solution.py:26
  158.2 2.0 %convert_add_fusion = f32[1536,256]{1,0:T(8,128)S(1)} fusion(bf16[1536,256]{1,0:T(8,128)(2,1)S(1)} %collective-permute-done.26, bf16[1536,256]{1,0:T(8,128)(2,1)} %collective-permute-done.25, bf16[1536,256]{1,0:T(8,128)(2,1)} %collective-permute-done.24, bf16[1536,256]{1,0:T(8,128)(2,1)} %convolution_convert_fusion.2), kind=kLoop, calls=%fused_computation.15 | loop fusion | flops 2752512 | bytes 4718592 | tf_op jit(solution)/shard_map/add | solution.py:143
  160.3 1.0 collective-permute-start.27
  161.3 3.8 %convolution_add_fusion = f32[384,1848]{0,1:T(8,128)S(1)} fusion(bf16[1848,1024]{1,0:T(8,128)(2,1)S(1)} %copy-done.4, bf16[768,1848]{0,1:T(8,128)(2,1)} %collective-permute-done.20, bf16[1536,1024]{1,0:T(8,128)(2,1)} %copy-done.21), kind=kOutput, calls=%fused_computation.4 | convolution fusion | flops 1454745600 | bytes 8828928 | tf_op jit(solution)/shard_map/dot_general | solution.py:30
  165.1 3.9 %collective-permute-done.27 = bf16[1536,128]{1,0:T(8,128)(2,1)S(1)} collective-permute-done((bf16[1536,128]{1,0:T(8,128)(2,1)S(1)}, bf16[1536,128]{1,0:T(8,128)(2,1)S(1)}, u32[]{:S(2)}, u32[]{:S(2)}) %collective-permute-start.27) | collective-permute-done | bytes 393248 | tf_op jit(solution)/shard_map/ppermute | solution.py:18
  169.3 6.1 %collective-permute-start.30 = (bf16[384,128]{1,0:T(8,128)(2,1)S(1)}, bf16[384,128]{1,0:T(8,128)(2,1)S(1)}, u32[]{:S(2)}, u32[]{:S(2)}) collective-permute-start(bf16[384,128]{1,0:T(8,128)(2,1)S(1)} %get-tuple-element.93), channel_id=1, source_target_pairs={{24,0},{16,8},{8,16},{0,24},{25,1},{17,9},{9,17},{1,25},{26,2},{18... | collective-permute-start | bytes 294920 | tf_op jit(solution)/shard_map/ppermute | solution.py:26
  175.9 1.8 add_convert_fusion
  177.8 0.8 collective-permute-done.30
  178.6 2.1 %collective-permute-done.29 = bf16[384,128]{1,0:T(8,128)(2,1)S(1)} collective-permute-done((bf16[384,128]{1,0:T(8,128)(2,1)S(1)}, bf16[384,128]{1,0:T(8,128)(2,1)S(1)}, u32[]{:S(2)}, u32[]{:S(2)}) %collective-permute-start.29) | collective-permute-done | bytes 98336 | tf_op jit(solution)/shard_map/ppermute | solution.py:26
  180.8 0.8 pad_maximum_fusion.5
  (110 shorter events, 6.2 us)
Async XLA Ops:
  7.2 66.3 %copy-start = (bf16[16,1848]{1,0:T(8,128)(2,1)S(1)}, bf16[16,1848]{1,0:T(8,128)(2,1)}, u32[]{:S(2)}) copy-start(bf16[16,1848]{1,0:T(8,128)(2,1)} %param.7) | copy-start | bytes 177412
  7.2 63.3 %copy-start.5 = (bf16[384,1848]{0,1:T(8,128)(2,1)S(1)}, bf16[384,1848]{0,1:T(8,128)(2,1)}, u32[]{:S(2)}) copy-start(bf16[384,1848]{0,1:T(8,128)(2,1)} %param.5) | copy-start | bytes 4257796
  7.2 76.3 %all-gather.4.cloned.1.call-start = ((), (), s32[]{:S(2)}) async-start(), calls=%async_computation | async-start | bytes 4257792 | tf_op jit(solution)/shard_map/all_gather | solution.py:76
  7.9 138.8 %all-gather.6.cloned.1.call-start = ((), (), s32[]{:S(2)}) async-start(), calls=%async_computation.1 | async-start | bytes 1400832 | tf_op jit(solution)/shard_map/all_gather | solution.py:127
  8.0 9.4 %collective-permute-start.5 = (bf16[16,128]{1,0:T(8,128)(2,1)}, bf16[16,128]{1,0:T(8,128)(2,1)S(1)}, u32[]{:S(2)}, u32[]{:S(2)}) collective-permute-start(bf16[16,128]{1,0:T(8,128)(2,1)} %param.8), channel_id=1, source_target_pairs={{24,0},{16,8},{8,16},{0,24},{25,1},{17,9},{9,17},{1,25},{26,2},{18... | collective-permute-start | bytes 12296 | tf_op jit(solution)/shard_map/ppermute | solution.py:26
  12.2 7.1 %collective-permute-start.4 = (bf16[16,128]{1,0:T(8,128)(2,1)}, bf16[16,128]{1,0:T(8,128)(2,1)S(1)}, u32[]{:S(2)}, u32[]{:S(2)}) collective-permute-start(bf16[16,128]{1,0:T(8,128)(2,1)} %param.8), channel_id=1, source_target_pairs={{16,0},{24,8},{0,16},{8,24},{17,1},{25,9},{1,17},{9,25},{18,2},{26... | collective-permute-start | bytes 12296 | tf_op jit(solution)/shard_map/ppermute | solution.py:26
  14.2 5.1 %collective-permute-start.3 = (bf16[16,128]{1,0:T(8,128)(2,1)}, bf16[16,128]{1,0:T(8,128)(2,1)S(1)}, u32[]{:S(2)}, u32[]{:S(2)}) collective-permute-start(bf16[16,128]{1,0:T(8,128)(2,1)} %param.8), channel_id=1, source_target_pairs={{8,0},{0,8},{24,16},{16,24},{9,1},{1,9},{25,17},{17,25},{10,2},{2,... | collective-permute-start | bytes 12296 | tf_op jit(solution)/shard_map/ppermute | solution.py:26
  15.9 8.6 %copy-start.20 = (bf16[384,128]{1,0:T(8,128)(2,1)}, bf16[384,128]{1,0:T(8,128)(2,1)S(1)}, u32[]{:S(2)}) copy-start(bf16[384,128]{1,0:T(8,128)(2,1)S(1)} %get-tuple-element.99) | copy-start | bytes 294916
  15.9 6.6 %collective-permute-start.2 = (bf16[384,128]{1,0:T(8,128)(2,1)S(1)}, bf16[384,128]{1,0:T(8,128)(2,1)S(1)}, u32[]{:S(2)}, u32[]{:S(2)}) collective-permute-start(bf16[384,128]{1,0:T(8,128)(2,1)S(1)} %get-tuple-element.99), channel_id=1, source_target_pairs={{24,0},{16,8},{8,16},{0,24},{25,1},{17,9},{9,17},{1,25},{26,2},{18... | collective-permute-start | bytes 294920 | tf_op jit(solution)/shard_map/ppermute | solution.py:26
  17.3 5.2 %collective-permute-start.1 = (bf16[384,128]{1,0:T(8,128)(2,1)}, bf16[384,128]{1,0:T(8,128)(2,1)S(1)}, u32[]{:S(2)}, u32[]{:S(2)}) collective-permute-start(bf16[384,128]{1,0:T(8,128)(2,1)} %get-tuple-element.97), channel_id=1, source_target_pairs={{8,0},{0,8},{24,16},{16,24},{9,1},{1,9},{25,17},{17,25},{10,2},{2,... | collective-permute-start | bytes 294920 | tf_op jit(solution)/shard_map/ppermute | solution.py:26
  17.4 7.1 %collective-permute-start = (bf16[384,128]{1,0:T(8,128)(2,1)}, bf16[384,128]{1,0:T(8,128)(2,1)S(1)}, u32[]{:S(2)}, u32[]{:S(2)}) collective-permute-start(bf16[384,128]{1,0:T(8,128)(2,1)} %get-tuple-element.98), channel_id=1, source_target_pairs={{16,0},{24,8},{0,16},{8,24},{17,1},{25,9},{1,17},{9,25},{18,2},{26... | collective-permute-start | bytes 294920 | tf_op jit(solution)/shard_map/ppermute | solution.py:26
  24.6 10.2 %collective-permute-start.6 = (bf16[1536,128]{1,0:T(8,128)(2,1)S(1)}, bf16[1536,128]{1,0:T(8,128)(2,1)S(1)}, u32[]{:S(2)}, u32[]{:S(2)}) collective-permute-start(bf16[1536,128]{1,0:T(8,128)(2,1)S(1)} %pad_maximum_fusion.3), channel_id=1, source_target_pairs={{0,4},{4,0},{1,5},{5,1},{2,6},{6,2},{3,7},{7,3},{8,12},{12,8},{9,1... | collective-permute-start | bytes 1179656 | tf_op jit(solution)/shard_map/ppermute | solution.py:18
  24.7 10.2 %collective-permute-start.7 = (bf16[1536,128]{1,0:T(8,128)(2,1)S(1)}, bf16[1536,128]{1,0:T(8,128)(2,1)S(1)}, u32[]{:S(2)}, u32[]{:S(2)}) collective-permute-start(bf16[1536,128]{1,0:T(8,128)(2,1)S(1)} %pad_maximum_fusion.3), channel_id=1, source_target_pairs={{1,0},{0,1},{3,2},{2,3},{5,4},{4,5},{7,6},{6,7},{9,8},{8,9},{11,10... | collective-permute-start | bytes 1179656 | tf_op jit(solution)/shard_map/ppermute | solution.py:26
  24.8 10.1 %collective-permute-start.8 = (bf16[1536,128]{1,0:T(8,128)(2,1)S(1)}, bf16[1536,128]{1,0:T(8,128)(2,1)S(1)}, u32[]{:S(2)}, u32[]{:S(2)}) collective-permute-start(bf16[1536,128]{1,0:T(8,128)(2,1)S(1)} %pad_maximum_fusion.3), channel_id=1, source_target_pairs={{3,0},{2,1},{1,2},{0,3},{7,4},{6,5},{5,6},{4,7},{11,8},{10,9},{9,1... | collective-permute-start | bytes 1179656 | tf_op jit(solution)/shard_map/ppermute | solution.py:26
  34.7 34.1 %copy-start.8 = (bf16[1536,128]{1,0:T(8,128)(2,1)}, bf16[1536,128]{1,0:T(8,128)(2,1)S(1)}, u32[]{:S(2)}) copy-start(bf16[1536,128]{1,0:T(8,128)(2,1)S(1)} %collective-permute-done.6) | copy-start | bytes 1179652
  34.8 0.8 copy-start.14
  35.6 0.8 copy-start.12
  36.4 34.1 %collective-permute-start.9 = (bf16[384,1848]{0,1:T(8,128)(2,1)}, bf16[384,1848]{0,1:T(8,128)(2,1)S(1)}, u32[]{:S(2)}, u32[]{:S(2)}) collective-permute-start(bf16[384,1848]{0,1:T(8,128)(2,1)} %param.5), channel_id=1, source_target_pairs={{0,16},{16,0},{1,17},{17,1},{2,18},{18,2},{3,19},{19,3},{4,20},{20... | collective-permute-start | bytes 4257800 | tf_op jit(solution)/shard_map/ppermute | solution.py:18
  39.2 29.6 %collective-permute-start.14 = (bf16[1536,256]{1,0:T(8,128)(2,1)S(1)}, bf16[1536,256]{1,0:T(8,128)(2,1)S(1)}, u32[]{:S(2)}, u32[]{:S(2)}) collective-permute-start(bf16[1536,256]{1,0:T(8,128)(2,1)S(1)} %pad_maximum_fusion.2), channel_id=1, source_target_pairs={{2,0},{3,1},{0,2},{1,3},{6,4},{7,5},{4,6},{5,7},{10,8},{11,9},{8,1... | collective-permute-start | bytes 2359304 | tf_op jit(solution)/shard_map/ppermute | solution.py:26
  40.8 7.4 %collective-permute-start.10 = (bf16[1,16,512]{2,1,0:T(8,128)(2,1)S(1)}, bf16[1,16,512]{2,1,0:T(8,128)(2,1)S(1)}, u32[]{:S(2)}, u32[]{:S(2)}) collective-permute-start(bf16[1,16,512]{2,1,0:T(8,128)(2,1)S(1)} %maximum_bitcast_fusion), channel_id=1, source_target_pairs={{32,0},{64,32},{96,64},{128,96},{160,128},{192,160},{224,192},{0,2... | collective-permute-start | bytes 49160 | tf_op jit(solution)/shard_map/ppermute | solution.py:22
  46.4 18.9 %collective-permute-start.13 = (bf16[1536,128]{1,0:T(8,128)(2,1)S(1)}, bf16[1536,128]{1,0:T(8,128)(2,1)S(1)}, u32[]{:S(2)}, u32[]{:S(2)}) collective-permute-start(bf16[1536,128]{1,0:T(8,128)(2,1)S(1)} %collective-permute-done.6), channel_id=1, source_target_pairs={{1,0},{0,1},{3,2},{2,3},{5,4},{4,5},{7,6},{6,7},{9,8},{8,9},{11,10... | collective-permute-start | bytes 1179656 | tf_op jit(solution)/shard_map/ppermute | solution.py:26
  47.5 21.3 %collective-permute-start.15 = (bf16[1536,128]{1,0:T(8,128)(2,1)S(1)}, bf16[1536,128]{1,0:T(8,128)(2,1)S(1)}, u32[]{:S(2)}, u32[]{:S(2)}) collective-permute-start(bf16[1536,128]{1,0:T(8,128)(2,1)S(1)} %collective-permute-done.6), channel_id=1, source_target_pairs={{3,0},{2,1},{1,2},{0,3},{7,4},{6,5},{5,6},{4,7},{11,8},{10,9},{9,1... | collective-permute-start | bytes 1179656 | tf_op jit(solution)/shard_map/ppermute | solution.py:26
  48.3 4.7 %collective-permute-start.11 = (bf16[2,16,512]{2,1,0:T(8,128)(2,1)S(1)}, bf16[2,16,512]{2,1,0:T(8,128)(2,1)S(1)}, u32[]{:S(2)}, u32[]{:S(2)}) collective-permute-start(bf16[2,16,512]{2,1,0:T(8,128)(2,1)S(1)} %pad_maximum_fusion.11), channel_id=1, source_target_pairs={{64,0},{96,32},{128,64},{160,96},{192,128},{224,160},{0,192},{32,2... | collective-permute-start | bytes 98312 | tf_op jit(solution)/shard_map/ppermute | solution.py:22
  53.0 7.3 %collective-permute-start.12 = (bf16[4,16,512]{2,1,0:T(8,128)(2,1)S(1)}, bf16[4,16,512]{2,1,0:T(8,128)(2,1)S(1)}, u32[]{:S(2)}, u32[]{:S(2)}) collective-permute-start(bf16[4,16,512]{2,1,0:T(8,128)(2,1)S(1)} %pad_maximum_fusion.8), channel_id=1, source_target_pairs={{128,0},{160,32},{192,64},{224,96},{0,128},{32,160},{64,192},{96,2... | collective-permute-start | bytes 196616 | tf_op jit(solution)/shard_map/ppermute | solution.py:22
  65.4 3.4 %copy-start.18 = (bf16[1536,128]{1,0:T(8,128)(2,1)}, bf16[1536,128]{1,0:T(8,128)(2,1)S(1)}, u32[]{:S(2)}) copy-start(bf16[1536,128]{1,0:T(8,128)(2,1)S(1)} %collective-permute-done.13) | copy-start | bytes 1179652
  68.8 0.8 copy-start.16
  69.6 0.9 copy-start.10
  72.3 17.3 %collective-permute-start.19 = (bf16[768,1848]{0,1:T(8,128)(2,1)}, bf16[768,1848]{0,1:T(8,128)(2,1)}, u32[]{:S(2)}, u32[]{:S(2)}) collective-permute-start(bf16[768,1848]{0,1:T(8,128)(2,1)} %pad_maximum_fusion.1), channel_id=1, source_target_pairs={{0,8},{8,0},{1,9},{9,1},{2,10},{10,2},{3,11},{11,3},{4,12},{12,4},... | collective-permute-start | bytes 8515592 | tf_op jit(solution)/shard_map/ppermute | solution.py:18
  73.5 2.4 %copy-start.9 = (bf16[1536,128]{1,0:T(8,128)(2,1)S(1)}, bf16[1536,128]{1,0:T(8,128)(2,1)}, u32[]{:S(2)}) copy-start(bf16[1536,128]{1,0:T(8,128)(2,1)} %copy-done.8) | copy-start | bytes 1179652
  73.5 2.5 %copy-start.15 = (bf16[1536,128]{1,0:T(8,128)(2,1)S(1)}, bf16[1536,128]{1,0:T(8,128)(2,1)}, u32[]{:S(2)}) copy-start(bf16[1536,128]{1,0:T(8,128)(2,1)} %copy-done.14) | copy-start | bytes 1179652
  73.5 2.7 %copy-start.19 = (bf16[1536,128]{1,0:T(8,128)(2,1)S(1)}, bf16[1536,128]{1,0:T(8,128)(2,1)}, u32[]{:S(2)}) copy-start(bf16[1536,128]{1,0:T(8,128)(2,1)} %copy-done.18) | copy-start | bytes 1179652
  73.5 2.8 %copy-start.11 = (bf16[1536,256]{1,0:T(8,128)(2,1)S(1)}, bf16[1536,256]{1,0:T(8,128)(2,1)}, u32[]{:S(2)}) copy-start(bf16[1536,256]{1,0:T(8,128)(2,1)} %copy-done.10) | copy-start | bytes 2359300
  73.8 2.6 %copy-start.13 = (bf16[1536,128]{1,0:T(8,128)(2,1)S(1)}, bf16[1536,128]{1,0:T(8,128)(2,1)}, u32[]{:S(2)}) copy-start(bf16[1536,128]{1,0:T(8,128)(2,1)} %copy-done.12) | copy-start | bytes 1179652
  73.9 2.7 %copy-start.17 = (bf16[1536,128]{1,0:T(8,128)(2,1)S(1)}, bf16[1536,128]{1,0:T(8,128)(2,1)}, u32[]{:S(2)}) copy-start(bf16[1536,128]{1,0:T(8,128)(2,1)} %copy-done.16) | copy-start | bytes 1179652
  75.3 3.6 %collective-permute-start.16 = (f32[32,384]{1,0:T(8,128)S(1)}, f32[32,384]{1,0:T(8,128)S(1)}, u32[]{:S(2)}, u32[]{:S(2)}) collective-permute-start(f32[32,384]{1,0:T(8,128)S(1)} %pad_maximum_fusion.9), channel_id=1, source_target_pairs={{1,0},{0,1},{3,2},{2,3},{5,4},{4,5},{7,6},{6,7},{9,8},{8,9},{11,10... | collective-permute-start | bytes 147464 | tf_op jit(solution)/shard_map/ppermute | solution.py:26
  76.8 2.1 %copy-start.21 = (bf16[1536,1024]{1,0:T(8,128)(2,1)}, bf16[1536,1024]{1,0:T(8,128)(2,1)S(1)}, u32[]{:S(2)}) copy-start(bf16[1536,1024]{1,0:T(8,128)(2,1)S(1)} %constant_dynamic-update-slice_fusion) | copy-start | bytes 9437188
  78.9 4.5 %collective-permute-start.17 = (f32[32,384]{1,0:T(8,128)S(1)}, f32[32,384]{1,0:T(8,128)S(1)}, u32[]{:S(2)}, u32[]{:S(2)}) collective-permute-start(f32[32,384]{1,0:T(8,128)S(1)} %fusion.24), channel_id=1, source_target_pairs={{2,0},{3,1},{0,2},{1,3},{6,4},{7,5},{4,6},{5,7},{10,8},{11,9},{8,1... | collective-permute-start | bytes 147464 | tf_op jit(solution)/shard_map/ppermute | solution.py:26
  83.5 2.1 %copy-start.1 = (bf16[1848,1024]{1,0:T(8,128)(2,1)S(1)}, bf16[1848,1024]{1,0:T(8,128)(2,1)}, u32[]{:S(2)}) copy-start(bf16[1848,1024]{1,0:T(8,128)(2,1)} %all-gather.4.cloned.1.call-done.in_ref) | copy-start | bytes 11354116
  88.5 17.6 %copy-start.2 = (bf16[1848,1024]{1,0:T(8,128)(2,1)}, bf16[1848,1024]{1,0:T(8,128)(2,1)S(1)}, u32[]{:S(2)}) copy-start(bf16[1848,1024]{1,0:T(8,128)(2,1)S(1)} %shard_map.84) | copy-start | bytes 11354116
  88.5 5.1 %copy-start.22 = (bf16[1536,1024]{1,0:T(8,128)(2,1)S(1)}, bf16[1536,1024]{1,0:T(8,128)(2,1)}, u32[]{:S(2)}) copy-start(bf16[1536,1024]{1,0:T(8,128)(2,1)} %copy-done.21) | copy-start | bytes 9437188
  88.5 5.0 %collective-permute-start.18 = (f32[32,384]{1,0:T(8,128)S(1)}, f32[32,384]{1,0:T(8,128)S(1)}, u32[]{:S(2)}, u32[]{:S(2)}) collective-permute-start(f32[32,384]{1,0:T(8,128)S(1)} %add.119), channel_id=1, source_target_pairs={{4,0},{5,1},{6,2},{7,3},{0,4},{1,5},{2,6},{3,7},{12,8},{13,9},{14,... | collective-permute-start | bytes 147464 | tf_op jit(solution)/shard_map/ppermute | solution.py:26
  93.6 12.5 %copy-start.6 = (bf16[1536,1848]{0,1:T(8,128)(2,1)}, bf16[1536,1848]{0,1:T(8,128)(2,1)S(1)}, u32[]{:S(2)}) copy-start(bf16[1536,1848]{0,1:T(8,128)(2,1)S(1)} %pad_maximum_fusion) | copy-start | bytes 17031172
  98.1 13.9 %collective-permute-start.20 = (bf16[768,1848]{0,1:T(8,128)(2,1)}, bf16[768,1848]{0,1:T(8,128)(2,1)}, u32[]{:S(2)}, u32[]{:S(2)}) collective-permute-start(bf16[768,1848]{0,1:T(8,128)(2,1)} %convolution_convert_fusion), channel_id=1, source_target_pairs={{0,8},{8,0},{1,9},{9,1},{2,10},{10,2},{3,11},{11,3},{4,12},{12,4},... | collective-permute-start | bytes 8515592 | tf_op jit(solution)/shard_map/ppermute | solution.py:18
  100.5 8.5 %collective-permute-start.21 = (bf16[16,384]{1,0:T(8,128)(2,1)S(1)}, bf16[16,384]{1,0:T(8,128)(2,1)S(1)}, u32[]{:S(2)}, u32[]{:S(2)}) collective-permute-start(bf16[16,384]{1,0:T(8,128)(2,1)S(1)} %slice.81), channel_id=1, source_target_pairs={{0,16},{16,0},{1,17},{17,1},{2,18},{18,2},{3,19},{19,3},{4,20},{20... | collective-permute-start | bytes 36872 | tf_op jit(solution)/shard_map/ppermute | solution.py:18
  106.1 2.8 %copy-start.7 = (bf16[384,512]{1,0:T(8,128)(2,1)S(1)}, bf16[384,512]{1,0:T(8,128)(2,1)}, u32[]{:S(2)}) copy-start(bf16[384,512]{1,0:T(8,128)(2,1)} %param.9) | copy-start | bytes 1179652
  109.1 1.3 collective-permute-start.22
  109.5 1.6 collective-permute-start.31
  111.9 6.4 %slice-start = ((s8[5677056]{0:T(1024)(128)(4,1)}), s8[1482752]{0:T(1024)(128)(4,1)S(1)}, s32[]{:S(2)}) async-start(s8[5677056]{0:T(1024)(128)(4,1)} %bitcast.27), calls=%async_computation.2 | async-start | bytes 2965504
  111.9 6.4 %copy-start.3 = (bf16[1848,1024]{1,0:T(8,128)(2,1)S(1)}, bf16[1848,1024]{1,0:T(8,128)(2,1)}, u32[]{:S(2)}) copy-start(bf16[1848,1024]{1,0:T(8,128)(2,1)} %copy-done.2) | copy-start | bytes 11354116
  112.0 6.4 %slice-start.1 = ((s8[5677056]{0:T(1024)(128)(4,1)}), s8[4194304]{0:T(1024)(128)(4,1)S(1)}, s32[]{:S(2)}) async-start(s8[5677056]{0:T(1024)(128)(4,1)} %bitcast.27), calls=%async_computation.3 | async-start | bytes 8388608
  118.1 37.9 %collective-permute-start.23 = (bf16[384,1848]{0,1:T(8,128)(2,1)}, bf16[384,1848]{0,1:T(8,128)(2,1)S(1)}, u32[]{:S(2)}, u32[]{:S(2)}) collective-permute-start(bf16[384,1848]{0,1:T(8,128)(2,1)} %fusion.1), channel_id=1, source_target_pairs={{0,16},{16,0},{1,17},{17,1},{2,18},{18,2},{3,19},{19,3},{4,20},{20... | collective-permute-start | bytes 4257800 | tf_op jit(solution)/shard_map/ppermute | solution.py:18
  121.2 34.8 %collective-permute-start.24 = (bf16[1536,256]{1,0:T(8,128)(2,1)}, bf16[1536,256]{1,0:T(8,128)(2,1)}, u32[]{:S(2)}, u32[]{:S(2)}) collective-permute-start(bf16[1536,256]{1,0:T(8,128)(2,1)} %convolution_convert_fusion.4), channel_id=1, source_target_pairs={{1,0},{0,1},{3,2},{2,3},{5,4},{4,5},{7,6},{6,7},{9,8},{8,9},{11,10... | collective-permute-start | bytes 2359304 | tf_op jit(solution)/shard_map/ppermute | solution.py:26
  121.4 34.6 %collective-permute-start.25 = (bf16[1536,256]{1,0:T(8,128)(2,1)}, bf16[1536,256]{1,0:T(8,128)(2,1)}, u32[]{:S(2)}, u32[]{:S(2)}) collective-permute-start(bf16[1536,256]{1,0:T(8,128)(2,1)} %convolution_convert_fusion.3), channel_id=1, source_target_pairs={{3,0},{2,1},{1,2},{0,3},{7,4},{6,5},{5,6},{4,7},{11,8},{10,9},{9,1... | collective-permute-start | bytes 2359304 | tf_op jit(solution)/shard_map/ppermute | solution.py:26
  125.7 32.5 %collective-permute-start.26 = (bf16[1536,256]{1,0:T(8,128)(2,1)}, bf16[1536,256]{1,0:T(8,128)(2,1)S(1)}, u32[]{:S(2)}, u32[]{:S(2)}) collective-permute-start(bf16[1536,256]{1,0:T(8,128)(2,1)} %convolution_convert_fusion.1), channel_id=1, source_target_pairs={{2,0},{3,1},{0,2},{1,3},{6,4},{7,5},{4,6},{5,7},{10,8},{11,9},{8,1... | collective-permute-start | bytes 2359304 | tf_op jit(solution)/shard_map/ppermute | solution.py:26
  148.1 13.2 %copy-start.4 = (bf16[1848,1024]{1,0:T(8,128)(2,1)S(1)}, bf16[1848,1024]{1,0:T(8,128)(2,1)}, u32[]{:S(2)}) copy-start(bf16[1848,1024]{1,0:T(8,128)(2,1)} %copy-done.2) | copy-start | bytes 11354116
  148.1 6.5 %collective-permute-start.32 = (f32[16,2360]{1,0:T(8,128)S(1)}, f32[16,2360]{1,0:T(8,128)S(1)}, u32[]{:S(2)}, u32[]{:S(2)}) collective-permute-start(f32[16,2360]{1,0:T(8,128)S(1)} %reduce_sum.9), channel_id=1, source_target_pairs={{0,16},{16,0},{1,17},{17,1},{2,18},{18,2},{3,19},{19,3},{4,20},{20... | collective-permute-start | bytes 453128 | tf_op jit(solution)/shard_map/ppermute | solution.py:18
  160.3 8.6 %collective-permute-start.27 = (bf16[1536,128]{1,0:T(8,128)(2,1)S(1)}, bf16[1536,128]{1,0:T(8,128)(2,1)S(1)}, u32[]{:S(2)}, u32[]{:S(2)}) collective-permute-start(bf16[1536,128]{1,0:T(8,128)(2,1)S(1)} %slice.122), channel_id=1, source_target_pairs={{0,4},{4,0},{1,5},{5,1},{2,6},{6,2},{3,7},{7,3},{8,12},{12,8},{9,1... | collective-permute-start | bytes 1179656 | tf_op jit(solution)/shard_map/ppermute | solution.py:18
  169.3 9.3 %collective-permute-start.30 = (bf16[384,128]{1,0:T(8,128)(2,1)S(1)}, bf16[384,128]{1,0:T(8,128)(2,1)S(1)}, u32[]{:S(2)}, u32[]{:S(2)}) collective-permute-start(bf16[384,128]{1,0:T(8,128)(2,1)S(1)} %get-tuple-element.93), channel_id=1, source_target_pairs={{24,0},{16,8},{8,16},{0,24},{25,1},{17,9},{9,17},{1,25},{26,2},{18... | collective-permute-start | bytes 294920 | tf_op jit(solution)/shard_map/ppermute | solution.py:26
  175.4 5.2 %collective-permute-start.29 = (bf16[384,128]{1,0:T(8,128)(2,1)S(1)}, bf16[384,128]{1,0:T(8,128)(2,1)S(1)}, u32[]{:S(2)}, u32[]{:S(2)}) collective-permute-start(bf16[384,128]{1,0:T(8,128)(2,1)S(1)} %get-tuple-element.94), channel_id=1, source_target_pairs={{16,0},{24,8},{0,16},{8,24},{17,1},{25,9},{1,17},{9,25},{18,2},{26... | collective-permute-start | bytes 294920 | tf_op jit(solution)/shard_map/ppermute | solution.py:26
  175.5 5.2 %collective-permute-start.28 = (bf16[384,128]{1,0:T(8,128)(2,1)S(1)}, bf16[384,128]{1,0:T(8,128)(2,1)S(1)}, u32[]{:S(2)}, u32[]{:S(2)}) collective-permute-start(bf16[384,128]{1,0:T(8,128)(2,1)S(1)} %get-tuple-element.95), channel_id=1, source_target_pairs={{8,0},{0,8},{24,16},{16,24},{9,1},{1,9},{25,17},{17,25},{10,2},{2,... | collective-permute-start | bytes 294920 | tf_op jit(solution)/shard_map/ppermute | solution.py:26
Sparse Core Ops, SparseCore 0:
  9.7 66.8 all-gather.3
  112.1 34.6 all-gather.5

commit v2 on v1

--- a/solution.py
+++ b/solution.py
@@ -123,24 +123,26 @@
     rank, back = ranks[:16], ranks[16:]
     c = SCALE / math.sqrt(tokens * 32)
     grads = jnp.concatenate([c * dot(back, hidden, 1, 0), c * dot(rank, cot, 1, 0)], 1)
+    got, shares, cots, all_hidden = together((got, shares, cots, all_hidden))
+    sent = {k: from_xor(shares[k], "y", NY, k) for k in (1, 3)}
+    give = (backward(1, 2) + got[tokens:].astype(F32)).astype(BF16)
+    give, all_hidden, grads = together((give, all_hidden, grads))
     grads = grads + swap(grads, "core")
     all_grads = lax.all_gather(grads, "z", axis=0)
-    rank_x = jnp.concatenate([rank, swap(rank, "x_hi")], 1)
-    all_rank = jnp.concatenate([rank_x, swap(rank_x, "core")], 1)
-    got, shares, cots, all_hidden, all_rank = together((got, shares, cots, all_hidden, all_rank))
-    sent = {k: from_xor(shares[k], "y", NY, k) for k in (1, 3)}
-    give = (backward(1, 2) + got[tokens:].astype(F32)).astype(BF16)
-    give, all_hidden = together((give, all_hidden))
     last = swap(give, "x_hi")
     shares = together({2: forward(2), 0: forward(0)})
     sent[2] = from_xor(shares[2], "y", NY, 2)
-    main, last, sent[1], sent[3], cots = together((shares[0], last, sent[1], sent[3], cots))
-    grads = jnp.sum(all_grads, 0)
-    grads = grads + swap(grads, "x_hi")
+    last, sent[1], rank = together((last, sent[1], rank))
+    all_rank = [from_quad(rank, k) for k in range(1, 4)]
+    all_rank = jnp.concatenate([rank, all_rank[1], all_rank[0], all_rank[2]], 1)
+    main, sent[3], cots, all_rank = together((shares[0], sent[3], cots, all_rank))
 
     main = main.astype(F32)
     for k in (1, 3, 2):
         main = main + sent[k].astype(F32)
+    main, all_grads = together((main, all_grads))
+    grads = jnp.sum(all_grads, 0)
+    grads = grads + swap(grads, "x_hi")
     main = main[:, :group] + swap(main[:, group:].astype(BF16), "x_lo").astype(F32)
     out = (main + SCALE * dot(all_rank, factor[:, :group], 0, 0)).astype(BF16)
     rows = {0: 0, 2: 1, 1: 2, 3: 3}

time: 189 us -> 201 us (1.063); the launches traced: 188 us -> 197 us
  starting transfers between devices: 52.4 us -> 63.1 us
  waiting for transfers between devices: 67.4 us -> 62.5 us
  matrix products: 29.9 us -> 34.1 us
    all_gather x1, waiting for transfers between devices: 19.6 us -> 0.02 us  [local(): all_grads = lax.all_gather(grads, 'z', axis=0)]
    ppermute x20 -> x23, waiting for transfers between devices: 22.8 us -> 39.3 us  [from_xor(): return lax.ppermute(x, axis, [(i ^ k, i) for i in range(n)])]
    ppermute x10 -> x8, starting transfers between devices: 13.4 us -> 20.5 us  [swap(): return lax.ppermute(x, axis, [(0, 1), (1, 0)])]
    dot_general x13, matrix products: 29.9 us -> 34.1 us  [dot(): lax.dot_general(a, b, (((ca,), (cb,)), ((), ())), preferred_element_type=...]
    ppermute x20 -> x23, starting transfers between devices: 28.7 us -> 32.2 us  [from_xor(): return lax.ppermute(x, axis, [(i ^ k, i) for i in range(n)])]
    ppermute x10 -> x8, waiting for transfers between devices: 16.9 us -> 15 us  [swap(): return lax.ppermute(x, axis, [(0, 1), (1, 0)])]
    unnamed x56 -> x66, local copies, waits for them, and re-layouts: 5.99 us -> 5.8 us
  transfers between devices with their start and end apart: 35 -> 36, of which waited for: 18 -> 16; matrix products, arithmetic and copies ran while one was open for 20% -> 20% of each run, Pallas kernels for 2% -> 2%
where the time goes in v2:
time: 201 us; the launch traced here: 197 us
  starting transfers between devices  63.1 us (31%)
  waiting for transfers between devices  62.5 us (31%)
  matrix products  34.1 us (17%)
  between operations  14.7 us (7%)
  other arithmetic  10.1 us (5%)
  local copies, waits for them, and re-layouts  9.36 us (5%)
  Pallas kernels  2.98 us (1%)
    ppermute x23, waiting for transfers between devices, from_xor(): return lax.ppermute(x, axis, [(i ^ k, i) for i in range(n)])  39.3 us
    dot_general x13, matrix products, dot(): lax.dot_general(a, b, (((ca,), (cb,)), ((), ())), preferred_element_type=...  34.1 us
    ppermute x23, starting transfers between devices, from_xor(): return lax.ppermute(x, axis, [(i ^ k, i) for i in range(n)])  32.2 us
    ppermute x8, starting transfers between devices, swap(): return lax.ppermute(x, axis, [(0, 1), (1, 0)])  20.5 us
    ppermute x8, waiting for transfers between devices, swap(): return lax.ppermute(x, axis, [(0, 1), (1, 0)])  15 us
    ppermute x3, starting transfers between devices, from_offset(): return lax.ppermute(x, 'z', [((i + k) % NZ, i) for i in range(NZ)])  10.3 us
    ppermute x3, waiting for transfers between devices, from_offset(): return lax.ppermute(x, 'z', [((i + k) % NZ, i) for i in range(NZ)])  7.49 us
    unnamed x66, local copies, waits for them, and re-layouts  5.8 us
  transfers between devices with their start and end apart: 36, of which 16 were waited for; matrix products, arithmetic and copies ran while one was open for 20% of the time, Pallas kernels for 2%

profile of v2, /device:TPU:1, one launch (start us, length us, event | category | flops | bytes accessed | tf_op | source)
XLA Modules:
  0.0 196.9 jit_solution(1790114461366555090)
XLA Ops:
  7.2 0.7 all-gather.4.cloned.1.call-update
  8.0 4.2 %collective-permute-start.5 = (bf16[16,128]{1,0:T(8,128)(2,1)}, bf16[16,128]{1,0:T(8,128)(2,1)S(1)}, u32[]{:S(2)}, u32[]{:S(2)}) collective-permute-start(bf16[16,128]{1,0:T(8,128)(2,1)} %param.8), channel_id=1, source_target_pairs={{24,0},{16,8},{8,16},{0,24},{25,1},{17,9},{9,17},{1,25},{26,2},{18... | collective-permute-start | bytes 12296 | tf_op jit(solution)/shard_map/ppermute | solution.py:26
  12.2 2.0 collective-permute-start.4
  14.2 1.1 constant_dynamic-slice_fusion.7
  15.3 1.5 collective-permute-start.2
  16.9 1.9 collective-permute-start
  18.7 0.7 maximum_bitcast_fusion
  19.4 2.5 %collective-permute-done.2 = bf16[384,128]{1,0:T(8,128)(2,1)S(1)} collective-permute-done((bf16[384,128]{1,0:T(8,128)(2,1)S(1)}, bf16[384,128]{1,0:T(8,128)(2,1)S(1)}, u32[]{:S(2)}, u32[]{:S(2)}) %collective-permute-start.2) | collective-permute-done | bytes 98336 | tf_op jit(solution)/shard_map/ppermute | solution.py:26
  22.0 2.0 %collective-permute-done = bf16[384,128]{1,0:T(8,128)(2,1)S(1)} collective-permute-done((bf16[384,128]{1,0:T(8,128)(2,1)S(1)}, bf16[384,128]{1,0:T(8,128)(2,1)S(1)}, u32[]{:S(2)}, u32[]{:S(2)}) %collective-permute-start) | collective-permute-done | bytes 98336 | tf_op jit(solution)/shard_map/ppermute | solution.py:26
  24.4 1.9 collective-permute-start.8
  26.3 7.9 %collective-permute-done.6 = bf16[1536,128]{1,0:T(8,128)(2,1)S(1)} collective-permute-done((bf16[1536,128]{1,0:T(8,128)(2,1)S(1)}, bf16[1536,128]{1,0:T(8,128)(2,1)S(1)}, u32[]{:S(2)}, u32[]{:S(2)}) %collective-permute-start.6) | collective-permute-done | bytes 393248 | tf_op jit(solution)/shard_map/ppermute | solution.py:18
  35.1 0.7 copy-done.12
  35.8 2.7 %collective-permute-start.9 = (bf16[384,1848]{0,1:T(8,128)(2,1)}, bf16[384,1848]{0,1:T(8,128)(2,1)S(1)}, u32[]{:S(2)}, u32[]{:S(2)}) collective-permute-start(bf16[384,1848]{0,1:T(8,128)(2,1)} %param.5), channel_id=1, source_target_pairs={{0,16},{16,0},{1,17},{17,1},{2,18},{18,2},{3,19},{19,3},{4,20},{20... | collective-permute-start | bytes 4257800 | tf_op jit(solution)/shard_map/ppermute | solution.py:18
  38.7 1.6 collective-permute-start.14
  40.3 5.6 %collective-permute-start.10 = (bf16[1,16,512]{2,1,0:T(8,128)(2,1)S(1)}, bf16[1,16,512]{2,1,0:T(8,128)(2,1)S(1)}, u32[]{:S(2)}, u32[]{:S(2)}) collective-permute-start(bf16[1,16,512]{2,1,0:T(8,128)(2,1)S(1)} %maximum_bitcast_fusion), channel_id=1, source_target_pairs={{32,0},{64,32},{96,64},{128,96},{160,128},{192,160},{224,192},{0,2... | collective-permute-start | bytes 49160 | tf_op jit(solution)/shard_map/ppermute | solution.py:22
  45.9 1.0 collective-permute-start.13
  46.9 0.8 collective-permute-start.15
  47.7 1.8 collective-permute-start.11
  49.5 2.6 %collective-permute-done.11 = bf16[2,16,512]{2,1,0:T(8,128)(2,1)S(1)} collective-permute-done((bf16[2,16,512]{2,1,0:T(8,128)(2,1)S(1)}, bf16[2,16,512]{2,1,0:T(8,128)(2,1)S(1)}, u32[]{:S(2)}, u32[]{:S(2)}) %collective-permute-start.11) | collective-permute-done | bytes 32800 | tf_op jit(solution)/shard_map/ppermute | solution.py:22
  52.1 2.9 %collective-permute-start.12 = (bf16[4,16,512]{2,1,0:T(8,128)(2,1)S(1)}, bf16[4,16,512]{2,1,0:T(8,128)(2,1)S(1)}, u32[]{:S(2)}, u32[]{:S(2)}) collective-permute-start(bf16[4,16,512]{2,1,0:T(8,128)(2,1)S(1)} %pad_maximum_fusion.8), channel_id=1, source_target_pairs={{128,0},{160,32},{192,64},{224,96},{0,128},{32,160},{64,192},{96,2... | collective-permute-start | bytes 196616 | tf_op jit(solution)/shard_map/ppermute | solution.py:22
  55.0 4.9 %collective-permute-done.12 = bf16[4,16,512]{2,1,0:T(8,128)(2,1)S(1)} collective-permute-done((bf16[4,16,512]{2,1,0:T(8,128)(2,1)S(1)}, bf16[4,16,512]{2,1,0:T(8,128)(2,1)S(1)}, u32[]{:S(2)}, u32[]{:S(2)}) %collective-permute-start.12) | collective-permute-done | bytes 65568 | tf_op jit(solution)/shard_map/ppermute | solution.py:22
  59.9 4.9 %collective-permute-done.13 = bf16[1536,128]{1,0:T(8,128)(2,1)S(1)} collective-permute-done((bf16[1536,128]{1,0:T(8,128)(2,1)S(1)}, bf16[1536,128]{1,0:T(8,128)(2,1)S(1)}, u32[]{:S(2)}, u32[]{:S(2)}) %collective-permute-start.13) | collective-permute-done | bytes 393248 | tf_op jit(solution)/shard_map/ppermute | solution.py:26
  64.8 3.4 %collective-permute-done.15 = bf16[1536,128]{1,0:T(8,128)(2,1)S(1)} collective-permute-done((bf16[1536,128]{1,0:T(8,128)(2,1)S(1)}, bf16[1536,128]{1,0:T(8,128)(2,1)S(1)}, u32[]{:S(2)}, u32[]{:S(2)}) %collective-permute-start.15) | collective-permute-done | bytes 393248 | tf_op jit(solution)/shard_map/ppermute | solution.py:26
  68.3 0.7 copy-done.16
  69.0 0.9 copy-done.10
  69.9 1.9 pad_maximum_fusion.1
  71.8 1.2 collective-permute-start.19
  73.3 1.4 fusion.9
  74.7 0.7 collective-permute-start.16
  76.4 2.0 %collective-permute-done.16 = f32[32,384]{1,0:T(8,128)S(1)} collective-permute-done((f32[32,384]{1,0:T(8,128)S(1)}, f32[32,384]{1,0:T(8,128)S(1)}, u32[]{:S(2)}, u32[]{:S(2)}) %collective-permute-start.16) | collective-permute-done | bytes 49184 | tf_op jit(solution)/shard_map/ppermute | solution.py:26
  78.4 2.1 %collective-permute-start.17 = (f32[32,384]{1,0:T(8,128)S(1)}, f32[32,384]{1,0:T(8,128)S(1)}, u32[]{:S(2)}, u32[]{:S(2)}) collective-permute-start(f32[32,384]{1,0:T(8,128)S(1)} %fusion.22), channel_id=1, source_target_pairs={{2,0},{3,1},{0,2},{1,3},{6,4},{7,5},{4,6},{5,7},{10,8},{11,9},{8,1... | collective-permute-start | bytes 147464 | tf_op jit(solution)/shard_map/ppermute | solution.py:26
  80.6 2.3 %collective-permute-done.17 = f32[32,384]{1,0:T(8,128)S(1)} collective-permute-done((f32[32,384]{1,0:T(8,128)S(1)}, f32[32,384]{1,0:T(8,128)S(1)}, u32[]{:S(2)}, u32[]{:S(2)}) %collective-permute-start.17) | collective-permute-done | bytes 49184 | tf_op jit(solution)/shard_map/ppermute | solution.py:26
  83.0 2.1 %copy-done.1 = bf16[1848,1024]{1,0:T(8,128)(2,1)S(1)} copy-done((bf16[1848,1024]{1,0:T(8,128)(2,1)S(1)}, bf16[1848,1024]{1,0:T(8,128)(2,1)}, u32[]{:S(2)}) %copy-start.1) | copy-done | bytes 3784728
  85.0 3.0 %shard_map.84 = bf16[1848,1024]{1,0:T(8,128)(2,1)S(1)} custom-call(s32[8]{0:T(128)S(1)} %stack.35.at, bf16[1848,1024]{1,0:T(8,128)(2,1)S(1)} %copy-done.1), custom_call_target="tpu_custom_call" | custom-call | bytes 7569408 | tf_op jit(solution)/shard_map/pallas_call | solution.py:55
  88.0 1.1 collective-permute-start.18
  89.2 3.9 %pad_maximum_fusion = bf16[1536,1848]{0,1:T(8,128)(2,1)S(1)} fusion(bf16[768,1848]{0,1:T(8,128)(2,1)} %collective-permute-done.19, bf16[384,1848]{0,1:T(8,128)(2,1)S(1)} %collective-permute-done.9, bf16[384,1848]{0,1:T(8,128)(2,1)S(1)} %copy-done.3), kind=kLoop, calls=%fused_computation | loop fusion | flops 17031168 | bytes 11354112 | tf_op jit(solution)/shard_map/concatenate | solution.py:109
  93.1 3.4 %convolution_convert_fusion = bf16[768,1848]{0,1:T(8,128)(2,1)S(1)} fusion(bf16[1848,1024]{1,0:T(8,128)(2,1)S(1)} %shard_map.84, bf16[1536,1024]{1,0:T(8,128)(2,1)S(1)} %copy-done.24), kind=kOutput, calls=%fused_computation.1 | convolution fusion | flops 2908071936 | bytes 8196096 | tf_op jit(solution)/shard_map/dot_general | solution.py:30
  96.5 2.1 %collective-permute-start.20 = (bf16[768,1848]{0,1:T(8,128)(2,1)S(1)}, bf16[768,1848]{0,1:T(8,128)(2,1)S(1)}, u32[]{:S(2)}, u32[]{:S(2)}) collective-permute-start(bf16[768,1848]{0,1:T(8,128)(2,1)S(1)} %convolution_convert_fusion), channel_id=1, source_target_pairs={{0,8},{8,0},{1,9},{9,1},{2,10},{10,2},{3,11},{11,3},{4,12},{12,4},... | collective-permute-start | bytes 8515592 | tf_op jit(solution)/shard_map/ppermute | solution.py:18
  99.4 2.8 %convolution_convert_fusion.4 = bf16[1536,256]{1,0:T(8,128)(2,1)} fusion(bf16[1536,1848]{0,1:T(8,128)(2,1)S(1)} %pad_maximum_fusion, bf16[1848,1024]{1,0:T(8,128)(2,1)S(1)} %shard_map.84), kind=kOutput, calls=%fused_computation.12 | convolution fusion | flops 1453719552 | bytes 7409664 | tf_op jit(solution)/shard_map/dot_general | solution.py:30
  102.1 2.8 %convolution_convert_fusion.3 = bf16[1536,256]{1,0:T(8,128)(2,1)} fusion(bf16[1536,1848]{0,1:T(8,128)(2,1)S(1)} %pad_maximum_fusion, bf16[1848,1024]{1,0:T(8,128)(2,1)S(1)} %shard_map.84), kind=kOutput, calls=%fused_computation.11 | convolution fusion | flops 1453719552 | bytes 7409664 | tf_op jit(solution)/shard_map/dot_general | solution.py:30
  104.9 3.4 %fusion.1 = bf16[384,1848]{0,1:T(8,128)(2,1)} fusion(bf16[1848,1024]{1,0:T(8,128)(2,1)S(1)} %shard_map.84, bf16[768,1848]{0,1:T(8,128)(2,1)S(1)} %collective-permute-done.20, bf16[1536,1024]{1,0:T(8,128)(2,1)S(1)} %copy-done.24), kind=kOutput, calls=%fused_computation.8 | convolution fusion | flops 1455455232 | bytes 7409664 | tf_op jit(solution)/shard_map/dot_general | solution.py:30
  108.4 12.2 %collective-permute-start.22 = (bf16[384,1848]{0,1:T(8,128)(2,1)}, bf16[384,1848]{0,1:T(8,128)(2,1)S(1)}, u32[]{:S(2)}, u32[]{:S(2)}) collective-permute-start(bf16[384,1848]{0,1:T(8,128)(2,1)} %fusion.1), channel_id=1, source_target_pairs={{0,16},{16,0},{1,17},{17,1},{2,18},{18,2},{3,19},{19,3},{4,20},{20... | collective-permute-start | bytes 4257800 | tf_op jit(solution)/shard_map/ppermute | solution.py:18
  120.6 0.7 add.132
  121.3 4.9 %convolution_convert_fusion.2 = bf16[1536,256]{1,0:T(8,128)(2,1)S(1)} fusion(bf16[1536,1848]{0,1:T(8,128)(2,1)} %copy-done.4, bf16[1848,1024]{1,0:T(8,128)(2,1)} %copy-done.2), kind=kOutput, calls=%fused_computation.10 | convolution fusion | flops 1453719552 | bytes 7409664 | tf_op jit(solution)/shard_map/dot_general | solution.py:30
  126.4 3.1 %convolution_convert_fusion.1 = bf16[1536,256]{1,0:T(8,128)(2,1)S(1)} fusion(bf16[1536,1848]{0,1:T(8,128)(2,1)S(1)} %bitcast.28, bf16[1848,1024]{1,0:T(8,128)(2,1)} %copy-done.2), kind=kOutput, calls=%fused_computation.9 | convolution fusion | flops 1453719552 | bytes 7409664 | tf_op jit(solution)/shard_map/dot_general | solution.py:30
  129.6 2.0 %collective-permute-start.21 = (bf16[1536,256]{1,0:T(8,128)(2,1)S(1)}, bf16[1536,256]{1,0:T(8,128)(2,1)S(1)}, u32[]{:S(2)}, u32[]{:S(2)}) collective-permute-start(bf16[1536,256]{1,0:T(8,128)(2,1)S(1)} %copy-done.26), channel_id=1, source_target_pairs={{3,0},{2,1},{1,2},{0,3},{7,4},{6,5},{5,6},{4,7},{11,8},{10,9},{9,1... | collective-permute-start | bytes 2359304 | tf_op jit(solution)/shard_map/ppermute | solution.py:26
  131.6 1.2 collective-permute-start.27
  132.8 12.0 %collective-permute-done.23 = bf16[1536,256]{1,0:T(8,128)(2,1)S(1)} collective-permute-done((bf16[1536,256]{1,0:T(8,128)(2,1)S(1)}, bf16[1536,256]{1,0:T(8,128)(2,1)S(1)}, u32[]{:S(2)}, u32[]{:S(2)}) %collective-permute-start.23) | collective-permute-done | bytes 786464 | tf_op jit(solution)/shard_map/ppermute | solution.py:26
  144.8 7.0 %collective-permute-done.22 = bf16[384,1848]{0,1:T(8,128)(2,1)S(1)} collective-permute-done((bf16[384,1848]{0,1:T(8,128)(2,1)}, bf16[384,1848]{0,1:T(8,128)(2,1)S(1)}, u32[]{:S(2)}, u32[]{:S(2)}) %collective-permute-start.22) | collective-permute-done | bytes 1419296 | tf_op jit(solution)/shard_map/ppermute | solution.py:18
  151.8 3.9 %collective-permute-start.26 = (bf16[16,384]{1,0:T(8,128)(2,1)S(1)}, bf16[16,384]{1,0:T(8,128)(2,1)S(1)}, u32[]{:S(2)}, u32[]{:S(2)}) collective-permute-start(bf16[16,384]{1,0:T(8,128)(2,1)S(1)} %slice.82), channel_id=1, source_target_pairs={{24,0},{16,8},{8,16},{0,24},{25,1},{17,9},{9,17},{1,25},{26,2},{18... | collective-permute-start | bytes 36872 | tf_op jit(solution)/shard_map/ppermute | solution.py:26
  156.0 1.5 collective-permute-done.26
  157.5 2.6 %collective-permute-done.24 = bf16[16,384]{1,0:T(8,128)(2,1)S(1)} collective-permute-done((bf16[16,384]{1,0:T(8,128)(2,1)S(1)}, bf16[16,384]{1,0:T(8,128)(2,1)S(1)}, u32[]{:S(2)}, u32[]{:S(2)}) %collective-permute-start.24) | collective-permute-done | bytes 12320 | tf_op jit(solution)/shard_map/ppermute | solution.py:26
  160.1 5.7 %collective-permute-done.21 = bf16[1536,256]{1,0:T(8,128)(2,1)S(1)} collective-permute-done((bf16[1536,256]{1,0:T(8,128)(2,1)S(1)}, bf16[1536,256]{1,0:T(8,128)(2,1)S(1)}, u32[]{:S(2)}, u32[]{:S(2)}) %collective-permute-start.21) | collective-permute-done | bytes 786464 | tf_op jit(solution)/shard_map/ppermute | solution.py:26
  166.2 0.8 slice.117
  167.0 6.5 %convolution_add_fusion = f32[384,1848]{0,1:T(8,128)} fusion(bf16[1848,1024]{1,0:T(8,128)(2,1)} %copy-done.2, bf16[768,1848]{0,1:T(8,128)(2,1)} %copy-done.25, bf16[1536,1024]{1,0:T(8,128)(2,1)} %copy-done.23), kind=kOutput, calls=%fused_computation.4 | convolution fusion | flops 1454745600 | bytes 8828928 | tf_op jit(solution)/shard_map/dot_general | solution.py:30
  173.5 1.4 reduce_sum.9
  174.9 2.2 %collective-permute-start.33 = (f32[16,2360]{1,0:T(8,128)S(1)}, f32[16,2360]{1,0:T(8,128)S(1)}, u32[]{:S(2)}, u32[]{:S(2)}) collective-permute-start(f32[16,2360]{1,0:T(8,128)S(1)} %reduce_sum.9), channel_id=1, source_target_pairs={{0,16},{16,0},{1,17},{17,1},{2,18},{18,2},{3,19},{19,3},{4,20},{20... | collective-permute-start | bytes 453128 | tf_op jit(solution)/shard_map/ppermute | solution.py:18
  177.1 1.3 add_convert_fusion.1
  178.4 3.3 %collective-permute-start.32 = (bf16[384,128]{1,0:T(8,128)(2,1)S(1)}, bf16[384,128]{1,0:T(8,128)(2,1)S(1)}, u32[]{:S(2)}, u32[]{:S(2)}) collective-permute-start(bf16[384,128]{1,0:T(8,128)(2,1)S(1)} %get-tuple-element.101), channel_id=1, source_target_pairs={{24,0},{16,8},{8,16},{0,24},{25,1},{17,9},{9,17},{1,25},{26,2},{18... | collective-permute-start | bytes 294920 | tf_op jit(solution)/shard_map/ppermute | solution.py:26
  181.7 2.2 %collective-permute-start.31 = (bf16[384,128]{1,0:T(8,128)(2,1)S(1)}, bf16[384,128]{1,0:T(8,128)(2,1)S(1)}, u32[]{:S(2)}, u32[]{:S(2)}) collective-permute-start(bf16[384,128]{1,0:T(8,128)(2,1)S(1)} %get-tuple-element.102), channel_id=1, source_target_pairs={{16,0},{24,8},{0,16},{8,24},{17,1},{25,9},{1,17},{9,25},{18,2},{26... | collective-permute-start | bytes 294920 | tf_op jit(solution)/shard_map/ppermute | solution.py:26
  183.9 3.6 %add_convert_fusion = bf16[384,1848]{0,1:T(8,128)(2,1)} fusion(bf16[384,1848]{0,1:T(8,128)(2,1)S(1)} %copy-done.9, f32[384,1848]{0,1:T(8,128)} %convolution_add_fusion, bf16[16,1848]{1,0:T(8,128)(2,1)S(1)} %copy-done, bf16[32,384]{1,0:T(8,128)(2,1)S(1)} %add.127), kind=kOutput, calls=%fused_computation.7 | convolution fusion | flops 26256384 | bytes 5750784 | tf_op jit(solution)/shard_map/dot_general | solution.py:30
  187.5 0.7 slice.89
  188.2 0.7 slice.90
  189.0 0.8 pad_maximum_fusion.5
  (121 shorter events, 4.9 us)
Async XLA Ops:
  7.2 65.8 %copy-start = (bf16[16,1848]{1,0:T(8,128)(2,1)S(1)}, bf16[16,1848]{1,0:T(8,128)(2,1)}, u32[]{:S(2)}) copy-start(bf16[16,1848]{1,0:T(8,128)(2,1)} %param.7) | copy-start | bytes 177412
  7.2 62.7 %copy-start.3 = (bf16[384,1848]{0,1:T(8,128)(2,1)S(1)}, bf16[384,1848]{0,1:T(8,128)(2,1)}, u32[]{:S(2)}) copy-start(bf16[384,1848]{0,1:T(8,128)(2,1)} %param.5) | copy-start | bytes 4257796
  7.2 75.8 %all-gather.4.cloned.1.call-start = ((), (), s32[]{:S(2)}) async-start(), calls=%async_computation | async-start | bytes 4257792 | tf_op jit(solution)/shard_map/all_gather | solution.py:76
  7.9 158.2 %all-gather.6.cloned.1.call-start = ((), (), s32[]{:S(2)}) async-start(), calls=%async_computation.1 | async-start | bytes 1400832 | tf_op jit(solution)/shard_map/all_gather | solution.py:131
  8.0 8.9 %collective-permute-start.5 = (bf16[16,128]{1,0:T(8,128)(2,1)}, bf16[16,128]{1,0:T(8,128)(2,1)S(1)}, u32[]{:S(2)}, u32[]{:S(2)}) collective-permute-start(bf16[16,128]{1,0:T(8,128)(2,1)} %param.8), channel_id=1, source_target_pairs={{24,0},{16,8},{8,16},{0,24},{25,1},{17,9},{9,17},{1,25},{26,2},{18... | collective-permute-start | bytes 12296 | tf_op jit(solution)/shard_map/ppermute | solution.py:26
  12.2 6.5 %collective-permute-start.4 = (bf16[16,128]{1,0:T(8,128)(2,1)}, bf16[16,128]{1,0:T(8,128)(2,1)S(1)}, u32[]{:S(2)}, u32[]{:S(2)}) collective-permute-start(bf16[16,128]{1,0:T(8,128)(2,1)} %param.8), channel_id=1, source_target_pairs={{16,0},{24,8},{0,16},{8,24},{17,1},{25,9},{1,17},{9,25},{18,2},{26... | collective-permute-start | bytes 12296 | tf_op jit(solution)/shard_map/ppermute | solution.py:26
  14.2 4.6 %collective-permute-start.3 = (bf16[16,128]{1,0:T(8,128)(2,1)}, bf16[16,128]{1,0:T(8,128)(2,1)S(1)}, u32[]{:S(2)}, u32[]{:S(2)}) collective-permute-start(bf16[16,128]{1,0:T(8,128)(2,1)} %param.8), channel_id=1, source_target_pairs={{8,0},{0,8},{24,16},{16,24},{9,1},{1,9},{25,17},{17,25},{10,2},{2,... | collective-permute-start | bytes 12296 | tf_op jit(solution)/shard_map/ppermute | solution.py:26
  15.2 8.8 %copy-start.20 = (bf16[384,128]{1,0:T(8,128)(2,1)}, bf16[384,128]{1,0:T(8,128)(2,1)S(1)}, u32[]{:S(2)}) copy-start(bf16[384,128]{1,0:T(8,128)(2,1)S(1)} %get-tuple-element.105) | copy-start | bytes 294916
  15.2 8.7 %copy-start.21 = (bf16[384,128]{1,0:T(8,128)(2,1)}, bf16[384,128]{1,0:T(8,128)(2,1)S(1)}, u32[]{:S(2)}) copy-start(bf16[384,128]{1,0:T(8,128)(2,1)S(1)} %get-tuple-element.106) | copy-start | bytes 294916
  15.3 8.7 %copy-start.22 = (bf16[384,128]{1,0:T(8,128)(2,1)}, bf16[384,128]{1,0:T(8,128)(2,1)S(1)}, u32[]{:S(2)}) copy-start(bf16[384,128]{1,0:T(8,128)(2,1)S(1)} %get-tuple-element.107) | copy-start | bytes 294916
  15.3 6.7 %collective-permute-start.2 = (bf16[384,128]{1,0:T(8,128)(2,1)S(1)}, bf16[384,128]{1,0:T(8,128)(2,1)S(1)}, u32[]{:S(2)}, u32[]{:S(2)}) collective-permute-start(bf16[384,128]{1,0:T(8,128)(2,1)S(1)} %get-tuple-element.107), channel_id=1, source_target_pairs={{24,0},{16,8},{8,16},{0,24},{25,1},{17,9},{9,17},{1,25},{26,2},{18... | collective-permute-start | bytes 294920 | tf_op jit(solution)/shard_map/ppermute | solution.py:26
  16.8 5.2 %collective-permute-start.1 = (bf16[384,128]{1,0:T(8,128)(2,1)S(1)}, bf16[384,128]{1,0:T(8,128)(2,1)S(1)}, u32[]{:S(2)}, u32[]{:S(2)}) collective-permute-start(bf16[384,128]{1,0:T(8,128)(2,1)S(1)} %get-tuple-element.105), channel_id=1, source_target_pairs={{8,0},{0,8},{24,16},{16,24},{9,1},{1,9},{25,17},{17,25},{10,2},{2,... | collective-permute-start | bytes 294920 | tf_op jit(solution)/shard_map/ppermute | solution.py:26
  16.9 7.1 %collective-permute-start = (bf16[384,128]{1,0:T(8,128)(2,1)S(1)}, bf16[384,128]{1,0:T(8,128)(2,1)S(1)}, u32[]{:S(2)}, u32[]{:S(2)}) collective-permute-start(bf16[384,128]{1,0:T(8,128)(2,1)S(1)} %get-tuple-element.106), channel_id=1, source_target_pairs={{16,0},{24,8},{0,16},{8,24},{17,1},{25,9},{1,17},{9,25},{18,2},{26... | collective-permute-start | bytes 294920 | tf_op jit(solution)/shard_map/ppermute | solution.py:26
  24.0 10.2 %collective-permute-start.6 = (bf16[1536,128]{1,0:T(8,128)(2,1)S(1)}, bf16[1536,128]{1,0:T(8,128)(2,1)S(1)}, u32[]{:S(2)}, u32[]{:S(2)}) collective-permute-start(bf16[1536,128]{1,0:T(8,128)(2,1)S(1)} %pad_maximum_fusion.3), channel_id=1, source_target_pairs={{0,4},{4,0},{1,5},{5,1},{2,6},{6,2},{3,7},{7,3},{8,12},{12,8},{9,1... | collective-permute-start | bytes 1179656 | tf_op jit(solution)/shard_map/ppermute | solution.py:18
  24.1 10.2 %collective-permute-start.7 = (bf16[1536,128]{1,0:T(8,128)(2,1)S(1)}, bf16[1536,128]{1,0:T(8,128)(2,1)S(1)}, u32[]{:S(2)}, u32[]{:S(2)}) collective-permute-start(bf16[1536,128]{1,0:T(8,128)(2,1)S(1)} %pad_maximum_fusion.3), channel_id=1, source_target_pairs={{1,0},{0,1},{3,2},{2,3},{5,4},{4,5},{7,6},{6,7},{9,8},{8,9},{11,10... | collective-permute-start | bytes 1179656 | tf_op jit(solution)/shard_map/ppermute | solution.py:26
  24.4 10.2 %collective-permute-start.8 = (bf16[1536,128]{1,0:T(8,128)(2,1)S(1)}, bf16[1536,128]{1,0:T(8,128)(2,1)S(1)}, u32[]{:S(2)}, u32[]{:S(2)}) collective-permute-start(bf16[1536,128]{1,0:T(8,128)(2,1)S(1)} %pad_maximum_fusion.3), channel_id=1, source_target_pairs={{3,0},{2,1},{1,2},{0,3},{7,4},{6,5},{5,6},{4,7},{11,8},{10,9},{9,1... | collective-permute-start | bytes 1179656 | tf_op jit(solution)/shard_map/ppermute | solution.py:26
  34.2 34.1 %copy-start.6 = (bf16[1536,128]{1,0:T(8,128)(2,1)}, bf16[1536,128]{1,0:T(8,128)(2,1)S(1)}, u32[]{:S(2)}) copy-start(bf16[1536,128]{1,0:T(8,128)(2,1)S(1)} %collective-permute-done.6) | copy-start | bytes 1179652
  34.3 0.8 copy-start.14
  35.8 34.0 %collective-permute-start.9 = (bf16[384,1848]{0,1:T(8,128)(2,1)}, bf16[384,1848]{0,1:T(8,128)(2,1)S(1)}, u32[]{:S(2)}, u32[]{:S(2)}) collective-permute-start(bf16[384,1848]{0,1:T(8,128)(2,1)} %param.5), channel_id=1, source_target_pairs={{0,16},{16,0},{1,17},{17,1},{2,18},{18,2},{3,19},{19,3},{4,20},{20... | collective-permute-start | bytes 4257800 | tf_op jit(solution)/shard_map/ppermute | solution.py:18
  38.7 29.6 %collective-permute-start.14 = (bf16[1536,256]{1,0:T(8,128)(2,1)S(1)}, bf16[1536,256]{1,0:T(8,128)(2,1)S(1)}, u32[]{:S(2)}, u32[]{:S(2)}) collective-permute-start(bf16[1536,256]{1,0:T(8,128)(2,1)S(1)} %pad_maximum_fusion.2), channel_id=1, source_target_pairs={{2,0},{3,1},{0,2},{1,3},{6,4},{7,5},{4,6},{5,7},{10,8},{11,9},{8,1... | collective-permute-start | bytes 2359304 | tf_op jit(solution)/shard_map/ppermute | solution.py:26
  40.3 7.4 %collective-permute-start.10 = (bf16[1,16,512]{2,1,0:T(8,128)(2,1)S(1)}, bf16[1,16,512]{2,1,0:T(8,128)(2,1)S(1)}, u32[]{:S(2)}, u32[]{:S(2)}) collective-permute-start(bf16[1,16,512]{2,1,0:T(8,128)(2,1)S(1)} %maximum_bitcast_fusion), channel_id=1, source_target_pairs={{32,0},{64,32},{96,64},{128,96},{160,128},{192,160},{224,192},{0,2... | collective-permute-start | bytes 49160 | tf_op jit(solution)/shard_map/ppermute | solution.py:22
  45.9 18.9 %collective-permute-start.13 = (bf16[1536,128]{1,0:T(8,128)(2,1)S(1)}, bf16[1536,128]{1,0:T(8,128)(2,1)S(1)}, u32[]{:S(2)}, u32[]{:S(2)}) collective-permute-start(bf16[1536,128]{1,0:T(8,128)(2,1)S(1)} %collective-permute-done.6), channel_id=1, source_target_pairs={{1,0},{0,1},{3,2},{2,3},{5,4},{4,5},{7,6},{6,7},{9,8},{8,9},{11,10... | collective-permute-start | bytes 1179656 | tf_op jit(solution)/shard_map/ppermute | solution.py:26
  46.9 21.3 %collective-permute-start.15 = (bf16[1536,128]{1,0:T(8,128)(2,1)S(1)}, bf16[1536,128]{1,0:T(8,128)(2,1)S(1)}, u32[]{:S(2)}, u32[]{:S(2)}) collective-permute-start(bf16[1536,128]{1,0:T(8,128)(2,1)S(1)} %collective-permute-done.6), channel_id=1, source_target_pairs={{3,0},{2,1},{1,2},{0,3},{7,4},{6,5},{5,6},{4,7},{11,8},{10,9},{9,1... | collective-permute-start | bytes 1179656 | tf_op jit(solution)/shard_map/ppermute | solution.py:26
  47.7 4.4 %collective-permute-start.11 = (bf16[2,16,512]{2,1,0:T(8,128)(2,1)S(1)}, bf16[2,16,512]{2,1,0:T(8,128)(2,1)S(1)}, u32[]{:S(2)}, u32[]{:S(2)}) collective-permute-start(bf16[2,16,512]{2,1,0:T(8,128)(2,1)S(1)} %pad_maximum_fusion.11), channel_id=1, source_target_pairs={{64,0},{96,32},{128,64},{160,96},{192,128},{224,160},{0,192},{32,2... | collective-permute-start | bytes 98312 | tf_op jit(solution)/shard_map/ppermute | solution.py:22
  52.1 7.8 %collective-permute-start.12 = (bf16[4,16,512]{2,1,0:T(8,128)(2,1)S(1)}, bf16[4,16,512]{2,1,0:T(8,128)(2,1)S(1)}, u32[]{:S(2)}, u32[]{:S(2)}) collective-permute-start(bf16[4,16,512]{2,1,0:T(8,128)(2,1)S(1)} %pad_maximum_fusion.8), channel_id=1, source_target_pairs={{128,0},{160,32},{192,64},{224,96},{0,128},{32,160},{64,192},{96,2... | collective-permute-start | bytes 196616 | tf_op jit(solution)/shard_map/ppermute | solution.py:22
  64.8 3.4 %copy-start.18 = (bf16[1536,128]{1,0:T(8,128)(2,1)}, bf16[1536,128]{1,0:T(8,128)(2,1)S(1)}, u32[]{:S(2)}) copy-start(bf16[1536,128]{1,0:T(8,128)(2,1)S(1)} %collective-permute-done.13) | copy-start | bytes 1179652
  69.0 0.9 copy-start.10
  71.8 17.4 %collective-permute-start.19 = (bf16[768,1848]{0,1:T(8,128)(2,1)}, bf16[768,1848]{0,1:T(8,128)(2,1)}, u32[]{:S(2)}, u32[]{:S(2)}) collective-permute-start(bf16[768,1848]{0,1:T(8,128)(2,1)} %pad_maximum_fusion.1), channel_id=1, source_target_pairs={{0,8},{8,0},{1,9},{9,1},{2,10},{10,2},{3,11},{11,3},{4,12},{12,4},... | collective-permute-start | bytes 8515592 | tf_op jit(solution)/shard_map/ppermute | solution.py:18
  73.0 2.5 %copy-start.7 = (bf16[1536,128]{1,0:T(8,128)(2,1)S(1)}, bf16[1536,128]{1,0:T(8,128)(2,1)}, u32[]{:S(2)}) copy-start(bf16[1536,128]{1,0:T(8,128)(2,1)} %copy-done.6) | copy-start | bytes 1179652
  73.0 2.7 %copy-start.15 = (bf16[1536,128]{1,0:T(8,128)(2,1)S(1)}, bf16[1536,128]{1,0:T(8,128)(2,1)}, u32[]{:S(2)}) copy-start(bf16[1536,128]{1,0:T(8,128)(2,1)} %copy-done.14) | copy-start | bytes 1179652
  73.0 2.8 %copy-start.19 = (bf16[1536,128]{1,0:T(8,128)(2,1)S(1)}, bf16[1536,128]{1,0:T(8,128)(2,1)}, u32[]{:S(2)}) copy-start(bf16[1536,128]{1,0:T(8,128)(2,1)} %copy-done.18) | copy-start | bytes 1179652
  73.0 3.0 %copy-start.11 = (bf16[1536,256]{1,0:T(8,128)(2,1)S(1)}, bf16[1536,256]{1,0:T(8,128)(2,1)}, u32[]{:S(2)}) copy-start(bf16[1536,256]{1,0:T(8,128)(2,1)} %copy-done.10) | copy-start | bytes 2359300
  73.3 2.8 %copy-start.13 = (bf16[1536,128]{1,0:T(8,128)(2,1)S(1)}, bf16[1536,128]{1,0:T(8,128)(2,1)}, u32[]{:S(2)}) copy-start(bf16[1536,128]{1,0:T(8,128)(2,1)} %copy-done.12) | copy-start | bytes 1179652
  73.3 2.9 %copy-start.17 = (bf16[1536,128]{1,0:T(8,128)(2,1)S(1)}, bf16[1536,128]{1,0:T(8,128)(2,1)}, u32[]{:S(2)}) copy-start(bf16[1536,128]{1,0:T(8,128)(2,1)} %copy-done.16) | copy-start | bytes 1179652
  74.7 3.7 %collective-permute-start.16 = (f32[32,384]{1,0:T(8,128)S(1)}, f32[32,384]{1,0:T(8,128)S(1)}, u32[]{:S(2)}, u32[]{:S(2)}) collective-permute-start(f32[32,384]{1,0:T(8,128)S(1)} %pad_maximum_fusion.9), channel_id=1, source_target_pairs={{1,0},{0,1},{3,2},{2,3},{5,4},{4,5},{7,6},{6,7},{9,8},{8,9},{11,10... | collective-permute-start | bytes 147464 | tf_op jit(solution)/shard_map/ppermute | solution.py:26
  76.4 2.0 %copy-start.23 = (bf16[1536,1024]{1,0:T(8,128)(2,1)}, bf16[1536,1024]{1,0:T(8,128)(2,1)S(1)}, u32[]{:S(2)}) copy-start(bf16[1536,1024]{1,0:T(8,128)(2,1)S(1)} %constant_dynamic-update-slice_fusion) | copy-start | bytes 9437188
  78.4 4.5 %collective-permute-start.17 = (f32[32,384]{1,0:T(8,128)S(1)}, f32[32,384]{1,0:T(8,128)S(1)}, u32[]{:S(2)}, u32[]{:S(2)}) collective-permute-start(f32[32,384]{1,0:T(8,128)S(1)} %fusion.22), channel_id=1, source_target_pairs={{2,0},{3,1},{0,2},{1,3},{6,4},{7,5},{4,6},{5,7},{10,8},{11,9},{8,1... | collective-permute-start | bytes 147464 | tf_op jit(solution)/shard_map/ppermute | solution.py:26
  83.0 2.1 %copy-start.1 = (bf16[1848,1024]{1,0:T(8,128)(2,1)S(1)}, bf16[1848,1024]{1,0:T(8,128)(2,1)}, u32[]{:S(2)}) copy-start(bf16[1848,1024]{1,0:T(8,128)(2,1)} %all-gather.4.cloned.1.call-done.in_ref) | copy-start | bytes 11354116
  88.0 16.9 %copy-start.2 = (bf16[1848,1024]{1,0:T(8,128)(2,1)}, bf16[1848,1024]{1,0:T(8,128)(2,1)S(1)}, u32[]{:S(2)}) copy-start(bf16[1848,1024]{1,0:T(8,128)(2,1)S(1)} %shard_map.84) | copy-start | bytes 11354116
  88.0 5.1 %copy-start.24 = (bf16[1536,1024]{1,0:T(8,128)(2,1)S(1)}, bf16[1536,1024]{1,0:T(8,128)(2,1)}, u32[]{:S(2)}) copy-start(bf16[1536,1024]{1,0:T(8,128)(2,1)} %copy-done.23) | copy-start | bytes 9437188
  88.0 5.0 %collective-permute-start.18 = (f32[32,384]{1,0:T(8,128)S(1)}, f32[32,384]{1,0:T(8,128)S(1)}, u32[]{:S(2)}, u32[]{:S(2)}) collective-permute-start(f32[32,384]{1,0:T(8,128)S(1)} %add.119), channel_id=1, source_target_pairs={{4,0},{5,1},{6,2},{7,3},{0,4},{1,5},{2,6},{3,7},{12,8},{13,9},{14,... | collective-permute-start | bytes 147464 | tf_op jit(solution)/shard_map/ppermute | solution.py:26
  93.1 9.0 %copy-start.4 = (bf16[1536,1848]{0,1:T(8,128)(2,1)}, bf16[1536,1848]{0,1:T(8,128)(2,1)S(1)}, u32[]{:S(2)}) copy-start(bf16[1536,1848]{0,1:T(8,128)(2,1)S(1)} %pad_maximum_fusion) | copy-start | bytes 17031172
  93.1 5.5 %copy-start.5 = (bf16[384,512]{1,0:T(8,128)(2,1)S(1)}, bf16[384,512]{1,0:T(8,128)(2,1)}, u32[]{:S(2)}) copy-start(bf16[384,512]{1,0:T(8,128)(2,1)} %param.9) | copy-start | bytes 1179652
  96.5 8.4 %collective-permute-start.20 = (bf16[768,1848]{0,1:T(8,128)(2,1)S(1)}, bf16[768,1848]{0,1:T(8,128)(2,1)S(1)}, u32[]{:S(2)}, u32[]{:S(2)}) collective-permute-start(bf16[768,1848]{0,1:T(8,128)(2,1)S(1)} %convolution_convert_fusion), channel_id=1, source_target_pairs={{0,8},{8,0},{1,9},{9,1},{2,10},{10,2},{3,11},{11,3},{4,12},{12,4},... | collective-permute-start | bytes 8515592 | tf_op jit(solution)/shard_map/ppermute | solution.py:18
  104.9 3.4 %copy-start.25 = (bf16[768,1848]{0,1:T(8,128)(2,1)}, bf16[768,1848]{0,1:T(8,128)(2,1)S(1)}, u32[]{:S(2)}) copy-start(bf16[768,1848]{0,1:T(8,128)(2,1)S(1)} %collective-permute-done.20) | copy-start | bytes 8515588
  108.3 12.3 %collective-permute-start.28 = (f32[16,2360]{1,0:T(8,128)S(1)}, f32[16,2360]{1,0:T(8,128)S(1)}, u32[]{:S(2)}, u32[]{:S(2)}) collective-permute-start(f32[16,2360]{1,0:T(8,128)S(1)} %pad_maximum_fusion.6), channel_id=1, source_target_pairs={{0,8},{8,0},{1,9},{9,1},{2,10},{10,2},{3,11},{11,3},{4,12},{12,4},... | collective-permute-start | bytes 453128 | tf_op jit(solution)/shard_map/ppermute | solution.py:18
  108.4 43.4 %collective-permute-start.22 = (bf16[384,1848]{0,1:T(8,128)(2,1)}, bf16[384,1848]{0,1:T(8,128)(2,1)S(1)}, u32[]{:S(2)}, u32[]{:S(2)}) collective-permute-start(bf16[384,1848]{0,1:T(8,128)(2,1)} %fusion.1), channel_id=1, source_target_pairs={{0,16},{16,0},{1,17},{17,1},{2,18},{18,2},{3,19},{19,3},{4,20},{20... | collective-permute-start | bytes 4257800 | tf_op jit(solution)/shard_map/ppermute | solution.py:18
  120.6 5.8 %slice-start = ((s8[5677056]{0:T(1024)(128)(4,1)}), s8[1482752]{0:T(1024)(128)(4,1)S(1)}, s32[]{:S(2)}) async-start(s8[5677056]{0:T(1024)(128)(4,1)} %bitcast.27), calls=%async_computation.2 | async-start | bytes 2965504
  121.3 4.9 %copy-start.27 = (bf16[1536,256]{1,0:T(8,128)(2,1)S(1)}, bf16[1536,256]{1,0:T(8,128)(2,1)}, u32[]{:S(2)}) copy-start(bf16[1536,256]{1,0:T(8,128)(2,1)} %convolution_convert_fusion.4) | copy-start | bytes 2359300
  121.3 5.1 %slice-start.1 = ((s8[5677056]{0:T(1024)(128)(4,1)}), s8[4194304]{0:T(1024)(128)(4,1)S(1)}, s32[]{:S(2)}) async-start(s8[5677056]{0:T(1024)(128)(4,1)} %bitcast.27), calls=%async_computation.3 | async-start | bytes 8388608
  126.2 3.3 %copy-start.26 = (bf16[1536,256]{1,0:T(8,128)(2,1)S(1)}, bf16[1536,256]{1,0:T(8,128)(2,1)}, u32[]{:S(2)}) copy-start(bf16[1536,256]{1,0:T(8,128)(2,1)} %convolution_convert_fusion.3) | copy-start | bytes 2359300
  126.2 18.5 %collective-permute-start.23 = (bf16[1536,256]{1,0:T(8,128)(2,1)S(1)}, bf16[1536,256]{1,0:T(8,128)(2,1)S(1)}, u32[]{:S(2)}, u32[]{:S(2)}) collective-permute-start(bf16[1536,256]{1,0:T(8,128)(2,1)S(1)} %copy-done.27), channel_id=1, source_target_pairs={{1,0},{0,1},{3,2},{2,3},{5,4},{4,5},{7,6},{6,7},{9,8},{8,9},{11,10... | collective-permute-start | bytes 2359304 | tf_op jit(solution)/shard_map/ppermute | solution.py:26
  129.6 36.2 %collective-permute-start.21 = (bf16[1536,256]{1,0:T(8,128)(2,1)S(1)}, bf16[1536,256]{1,0:T(8,128)(2,1)S(1)}, u32[]{:S(2)}, u32[]{:S(2)}) collective-permute-start(bf16[1536,256]{1,0:T(8,128)(2,1)S(1)} %copy-done.26), channel_id=1, source_target_pairs={{3,0},{2,1},{1,2},{0,3},{7,4},{6,5},{5,6},{4,7},{11,8},{10,9},{9,1... | collective-permute-start | bytes 2359304 | tf_op jit(solution)/shard_map/ppermute | solution.py:26
  131.6 34.2 %collective-permute-start.27 = (bf16[1536,256]{1,0:T(8,128)(2,1)S(1)}, bf16[1536,256]{1,0:T(8,128)(2,1)S(1)}, u32[]{:S(2)}, u32[]{:S(2)}) collective-permute-start(bf16[1536,256]{1,0:T(8,128)(2,1)S(1)} %convolution_convert_fusion.1), channel_id=1, source_target_pairs={{2,0},{3,1},{0,2},{1,3},{6,4},{7,5},{4,6},{5,7},{10,8},{11,9},{8,1... | collective-permute-start | bytes 2359304 | tf_op jit(solution)/shard_map/ppermute | solution.py:26
  151.8 21.7 %copy-start.8 = (bf16[384,1848]{0,1:T(8,128)(2,1)}, bf16[384,1848]{0,1:T(8,128)(2,1)S(1)}, u32[]{:S(2)}) copy-start(bf16[384,1848]{0,1:T(8,128)(2,1)S(1)} %collective-permute-done.22) | copy-start | bytes 4257796
  151.8 5.7 %collective-permute-start.26 = (bf16[16,384]{1,0:T(8,128)(2,1)S(1)}, bf16[16,384]{1,0:T(8,128)(2,1)S(1)}, u32[]{:S(2)}, u32[]{:S(2)}) collective-permute-start(bf16[16,384]{1,0:T(8,128)(2,1)S(1)} %slice.82), channel_id=1, source_target_pairs={{24,0},{16,8},{8,16},{0,24},{25,1},{17,9},{9,17},{1,25},{26,2},{18... | collective-permute-start | bytes 36872 | tf_op jit(solution)/shard_map/ppermute | solution.py:26
  155.7 1.8 collective-permute-start.25
  155.7 4.3 %collective-permute-start.24 = (bf16[16,384]{1,0:T(8,128)(2,1)S(1)}, bf16[16,384]{1,0:T(8,128)(2,1)S(1)}, u32[]{:S(2)}, u32[]{:S(2)}) collective-permute-start(bf16[16,384]{1,0:T(8,128)(2,1)S(1)} %slice.82), channel_id=1, source_target_pairs={{16,0},{24,8},{0,16},{8,24},{17,1},{25,9},{1,17},{9,25},{18,2},{26... | collective-permute-start | bytes 36872 | tf_op jit(solution)/shard_map/ppermute | solution.py:26
  167.0 10.1 %collective-permute-start.29 = (bf16[1536,128]{1,0:T(8,128)(2,1)}, bf16[1536,128]{1,0:T(8,128)(2,1)}, u32[]{:S(2)}, u32[]{:S(2)}) collective-permute-start(bf16[1536,128]{1,0:T(8,128)(2,1)} %slice.117), channel_id=1, source_target_pairs={{0,4},{4,0},{1,5},{5,1},{2,6},{6,2},{3,7},{7,3},{8,12},{12,8},{9,1... | collective-permute-start | bytes 1179656 | tf_op jit(solution)/shard_map/ppermute | solution.py:18
  174.8 9.0 %copy-start.9 = (bf16[384,1848]{0,1:T(8,128)(2,1)S(1)}, bf16[384,1848]{0,1:T(8,128)(2,1)}, u32[]{:S(2)}) copy-start(bf16[384,1848]{0,1:T(8,128)(2,1)} %copy-done.8) | copy-start | bytes 4257796
  174.9 12.7 %collective-permute-start.33 = (f32[16,2360]{1,0:T(8,128)S(1)}, f32[16,2360]{1,0:T(8,128)S(1)}, u32[]{:S(2)}, u32[]{:S(2)}) collective-permute-start(f32[16,2360]{1,0:T(8,128)S(1)} %reduce_sum.9), channel_id=1, source_target_pairs={{0,16},{16,0},{1,17},{17,1},{2,18},{18,2},{3,19},{19,3},{4,20},{20... | collective-permute-start | bytes 453128 | tf_op jit(solution)/shard_map/ppermute | solution.py:18
  178.4 10.5 %collective-permute-start.32 = (bf16[384,128]{1,0:T(8,128)(2,1)S(1)}, bf16[384,128]{1,0:T(8,128)(2,1)S(1)}, u32[]{:S(2)}, u32[]{:S(2)}) collective-permute-start(bf16[384,128]{1,0:T(8,128)(2,1)S(1)} %get-tuple-element.101), channel_id=1, source_target_pairs={{24,0},{16,8},{8,16},{0,24},{25,1},{17,9},{9,17},{1,25},{26,2},{18... | collective-permute-start | bytes 294920 | tf_op jit(solution)/shard_map/ppermute | solution.py:26
  181.7 7.2 %collective-permute-start.31 = (bf16[384,128]{1,0:T(8,128)(2,1)S(1)}, bf16[384,128]{1,0:T(8,128)(2,1)S(1)}, u32[]{:S(2)}, u32[]{:S(2)}) collective-permute-start(bf16[384,128]{1,0:T(8,128)(2,1)S(1)} %get-tuple-element.102), channel_id=1, source_target_pairs={{16,0},{24,8},{0,16},{8,24},{17,1},{25,9},{1,17},{9,25},{18,2},{26... | collective-permute-start | bytes 294920 | tf_op jit(solution)/shard_map/ppermute | solution.py:26
  183.9 5.0 %collective-permute-start.30 = (bf16[384,128]{1,0:T(8,128)(2,1)S(1)}, bf16[384,128]{1,0:T(8,128)(2,1)S(1)}, u32[]{:S(2)}, u32[]{:S(2)}) collective-permute-start(bf16[384,128]{1,0:T(8,128)(2,1)S(1)} %get-tuple-element.103), channel_id=1, source_target_pairs={{8,0},{0,8},{24,16},{16,24},{9,1},{1,9},{25,17},{17,25},{10,2},{2,... | collective-permute-start | bytes 294920 | tf_op jit(solution)/shard_map/ppermute | solution.py:26
  (2 other events, 1.5 us)
Sparse Core Ops, SparseCore 0:
  9.7 63.5 all-gather.3
  121.4 34.8 all-gather.5
